TPU v7x, 512 devices: a whole 4x4x16 slice. The times are simulated.
512 devices in a mesh: row: 32 (over z, core), col: 16 (over y, x).
Axes of the slice: x: 4, y: 4, z: 16, core: 2. Of those that a mesh axis runs over, the one named last changes fastest.
Arguments:
- demo: bfloat16 [32768, 256], P(('row', 'col'))
- rollout: bfloat16 [32768, 256], P(('row', 'col'))
Outputs:
- demo_potential: float32 [32768], P(('row', 'col'))
- rollout_potential: float32 [32768], P(('row', 'col'))
- rollout_reward: float32 [32768], P(('row', 'col'))
All inputs are finite; a program needn't handle non-finite values.
Results may differ from a plain program's by a relative error of at most 0.0065.
The roundings to bfloat16 on the way count: a program that leaves them out, or rounds other values in their place, can miss the bound.
Values may be sent and summed in bfloat16 or wider, within the bound.
No kernel may reach another device: no remote copies, remote signals or barrier semaphores. Data moves between devices by JAX's collectives and lax.ppermute only.
A program may use at most 64 MiB of HBM per device.

v0:
```python
import math

import jax
import jax.numpy as jnp
from jax import lax
from jax.sharding import PartitionSpec as P

ITERS = 2


EPS = 0.005


def normalize(embed):
    values = embed.astype(jnp.float32)
    inverse = lax.rsqrt(jnp.sum(values * values, axis=-1, keepdims=True) + 1e-06)
    return (values * inverse).astype(jnp.bfloat16)


def cost_of(left, right):
    inner = lax.dot_general(
        left, right, (((1,), (1,)), ((), ())), preferred_element_type=jnp.float32
    )
    return 1.0 - inner


def over_columns(expo):
    top = jnp.max(expo, axis=1)
    top = lax.pmax(top, "col")
    total = lax.psum(jnp.sum(jnp.exp(expo - top[:, None]), axis=1), "col")
    return top + jnp.log(total)


def over_rows(expo):
    top = jnp.max(expo, axis=0)
    top = lax.pmax(top, "row")
    total = lax.psum(jnp.sum(jnp.exp(expo - top[None, :]), axis=0), "row")
    return top + jnp.log(total)


def body(demo, rollout):
    demo_unit = lax.all_gather(normalize(demo), "col", axis=0, tiled=True)
    rollout_unit = lax.all_gather(normalize(rollout), "row", axis=0, tiled=True)
    rows_here = demo_unit.shape[0]
    cols_here = rollout_unit.shape[0]
    total_rows = rows_here * lax.axis_size("row")
    total_cols = cols_here * lax.axis_size("col")
    log_rows = -math.log(total_rows)
    log_cols = -math.log(total_cols)
    stored = cost_of(demo_unit, rollout_unit)

    def get_tile():
        return stored

    g_pot = jnp.zeros((cols_here,), jnp.float32)
    f_pot = jnp.zeros((rows_here,), jnp.float32)
    for step in range(ITERS):
        f_pot = EPS * log_rows - EPS * over_columns((g_pot[None, :] - get_tile()) / EPS)
        g_pot = EPS * log_cols - EPS * over_rows((f_pot[:, None] - get_tile()) / EPS)
    tile = get_tile()
    plan = jnp.exp((f_pot[:, None] + g_pot[None, :] - tile) / EPS)
    weighted = lax.psum(jnp.sum(plan * tile, axis=0), "row")
    reward = -float(total_cols) * weighted
    row_share = rows_here // lax.axis_size("col")
    col_share = cols_here // lax.axis_size("row")
    demo_out = lax.dynamic_slice_in_dim(f_pot / EPS, lax.axis_index("col") * row_share, row_share)
    rollout_out = lax.dynamic_slice_in_dim(
        g_pot / EPS, lax.axis_index("row") * col_share, col_share
    )
    reward_out = lax.dynamic_slice_in_dim(reward, lax.axis_index("row") * col_share, col_share)
    return (demo_out, rollout_out, reward_out)


def solution(mesh):
    return jax.shard_map(
        body,
        mesh=mesh,
        in_specs=(P(("row", "col"), None), P(("row", "col"), None)),
        out_specs=(P(("row", "col")), P(("row", "col")), P(("row", "col"))),
        check_vma=False,
    )
```

profile of v0, /device:TPU:1, one launch (start us, length us, event | category | flops | bytes accessed | tf_op | source)
XLA Modules:
  0.0 520.6 jit_solution(17992524907893724485)
XLA Ops:
  7.2 0.0 all-gather.2.cloned.1.call-start
  7.2 0.9 fusion.6
  8.1 1.4 fusion.7
  9.5 0.0 all-gather.2.cloned.1.call-update
  9.6 0.9 fusion.4
  10.4 0.8 fusion.5
  11.3 20.0 %all_gather.6 = bf16[1024,256]{1,0:T(8,128)(2,1)S(1)} all-gather(bf16[64,256]{1,0:T(8,128)(2,1)S(1)} %fusion.5), channel_id=1, replica_groups=mesh['row'=32,'col'=16] {'col'}, dimensions={0}, use_global_device_ids=true | all-gather | bytes 557056 | tf_op jit(solution)/shard_map/all_gather | solution.py:42
  31.3 55.2 %all-gather.2.cloned.1.call-done = bf16[2048,256]{1,0:T(8,128)(2,1)} async-done(((bf16[64,256]{1,0:T(8,128)(2,1)}), bf16[2048,256]{1,0:T(8,128)(2,1)}) %all-gather.2.cloned.1.call-update) | async-done | bytes 1048592 | tf_op jit(solution)/shard_map/all_gather | solution.py:43
  86.5 5.7 %fusion = (f32[1024]{0:T(1024)S(1)}, f32[1024,2048]{1,0:T(8,128)}) fusion(bf16[1024,256]{1,0:T(8,128)(2,1)S(1)} %all_gather.6, bf16[2048,256]{1,0:T(8,128)(2,1)} %all-gather.2.cloned.1.call-done), kind=kOutput, calls=%fused_computation.9 | convolution fusion | flops 1082129408 | bytes 9965568 | tf_op jit(solution)/shard_map/dot_general | solution.py:21
  92.3 33.2 %pmax.28 = f32[1024]{0:T(1024)S(1)} all-reduce(f32[1024]{0:T(1024)S(1)} %get-tuple-element.5), channel_id=1, replica_groups=mesh['row'=32,'col'=16] {'col'}, use_global_device_ids=true, to_apply=%region_3.0 | all-reduce | flops 1024 | bytes 8192 | tf_op jit(solution)/shard_map/pmax | solution.py:29
  125.5 4.6 exponential_reduce_fusion.3
  130.1 28.8 %psum.35 = f32[1024]{0:T(1024)S(1)} all-reduce(f32[1024]{0:T(1024)S(1)} %exponential_reduce_fusion.3), channel_id=1, replica_groups=mesh['row'=32,'col'=16] {'col'}, use_global_device_ids=true, to_apply=%region_5.0 | all-reduce | flops 1024 | bytes 8192 | tf_op jit(solution)/shard_map/psum | solution.py:30
  159.0 4.5 fusion.1
  163.5 60.1 %pmax.29 = f32[2048]{0:T(1024)S(1)} all-reduce(f32[2048]{0:T(1024)S(1)} %fusion.1), channel_id=1, replica_groups=mesh['row'=32,'col'=16] {'row'}, use_global_device_ids=true, to_apply=%region_7.0 | all-reduce | flops 2048 | bytes 16384 | tf_op jit(solution)/shard_map/pmax | solution.py:36
  223.6 4.6 exponential_reduce_fusion.2
  228.3 46.8 %psum.36 = f32[2048]{0:T(1024)S(1)} all-reduce(f32[2048]{0:T(1024)S(1)} %exponential_reduce_fusion.2), channel_id=1, replica_groups=mesh['row'=32,'col'=16] {'row'}, use_global_device_ids=true, to_apply=%region_9.0 | all-reduce | flops 2048 | bytes 16384 | tf_op jit(solution)/shard_map/psum | solution.py:37
  275.1 4.5 fusion.2
  279.7 30.3 %pmax.30 = f32[1024]{0:T(1024)S(1)} all-reduce(f32[1024]{0:T(1024)S(1)} %fusion.2), channel_id=1, replica_groups=mesh['row'=32,'col'=16] {'col'}, use_global_device_ids=true, to_apply=%region_11.0 | all-reduce | flops 1024 | bytes 8192 | tf_op jit(solution)/shard_map/pmax | solution.py:29
  309.9 4.6 exponential_reduce_fusion.1
  314.5 28.5 %psum.37 = f32[1024]{0:T(1024)S(1)} all-reduce(f32[1024]{0:T(1024)S(1)} %exponential_reduce_fusion.1), channel_id=1, replica_groups=mesh['row'=32,'col'=16] {'col'}, use_global_device_ids=true, to_apply=%region_13.0 | all-reduce | flops 1024 | bytes 8192 | tf_op jit(solution)/shard_map/psum | solution.py:30
  343.1 4.5 fusion.3
  347.6 61.0 %pmax.31 = f32[2048]{0:T(1024)S(1)} all-reduce(f32[2048]{0:T(1024)S(1)} %fusion.3), channel_id=1, replica_groups=mesh['row'=32,'col'=16] {'row'}, use_global_device_ids=true, to_apply=%region_15.0 | all-reduce | flops 2048 | bytes 16384 | tf_op jit(solution)/shard_map/pmax | solution.py:36
  408.6 4.6 exponential_reduce_fusion
  413.3 46.8 %psum.38 = f32[2048]{0:T(1024)S(1)} all-reduce(f32[2048]{0:T(1024)S(1)} %exponential_reduce_fusion), channel_id=1, replica_groups=mesh['row'=32,'col'=16] {'row'}, use_global_device_ids=true, to_apply=%region_17.0 | all-reduce | flops 2048 | bytes 16384 | tf_op jit(solution)/shard_map/psum | solution.py:37
  460.1 5.1 multiply_reduce_fusion
  465.2 46.8 %psum.39 = f32[2048]{0:T(1024)S(1)} all-reduce(f32[2048]{0:T(1024)S(1)} %multiply_reduce_fusion), channel_id=1, replica_groups=mesh['row'=32,'col'=16] {'row'}, use_global_device_ids=true, to_apply=%region_19.0 | all-reduce | flops 2048 | bytes 16384 | tf_op jit(solution)/shard_map/psum | solution.py:62
  512.0 0.6 dynamic-slice_multiply_fusion.1
  512.6 0.6 dynamic-slice_multiply_fusion
  513.2 0.6 dynamic_slice.9
  (6 shorter events, 0.1 us)
Async XLA Ops:
  7.2 79.4 %all-gather.2.cloned.1.call-start = ((), (), s32[]{:S(2)}) async-start(), calls=%async_computation | async-start | bytes 1081344 | tf_op jit(solution)/shard_map/all_gather | solution.py:43
Sparse Core Ops, SparseCore 0:
  10.1 76.3 all-gather.1
where the time goes:
time: 521 us
  blocking collectives  402 us (77%)
  waiting for transfers between devices  55.3 us (11%)
  other arithmetic  42.5 us (8%)
  between operations  14.2 us (3%)
  matrix products  5.74 us (1%)
    pmax x2, blocking collectives, over_rows(): top = lax.pmax(top, 'row')  121 us
    psum x2, blocking collectives, over_rows(): total = lax.psum(jnp.sum(jnp.exp(expo - top[None, :]), axis=0), 'row')  93.6 us
    pmax x2, blocking collectives, over_columns(): top = lax.pmax(top, 'col')  63.5 us
    psum x2, blocking collectives, over_columns(): total = lax.psum(jnp.sum(jnp.exp(expo - top[:, None]), axis=1), 'col')  57.3 us
    all_gather x1, waiting for transfers between devices, body(): rollout_unit = lax.all_gather(normalize(rollout), 'row', axis=0, tiled=True)  55.2 us
    psum x1, blocking collectives, body(): weighted = lax.psum(jnp.sum(plan * tile, axis=0), 'row')  46.8 us
    all_gather x1, blocking collectives, body(): demo_unit = lax.all_gather(normalize(demo), 'col', axis=0, tiled=True)  20 us
  transfers between devices with their start and end apart: 1, of which 1 were waited for; matrix products, arithmetic and copies ran while one was open for 0% of the time, Pallas kernels for 0%

commit v1 on v0

v1 whole, which is shorter than its diff:
```python
import functools
import math

import jax
import jax.numpy as jnp
from jax import lax
from jax.experimental import pallas as pl
from jax.experimental.pallas import tpu as pltpu
from jax.sharding import Mesh
from jax.sharding import PartitionSpec as P

EPS = 0.005
SCALE = 1.0 / (EPS * math.log(2.0))
LN2 = math.log(2.0)
LANES = 128
CHUNK = 256
PLANE = ("y", "x")
SHEET = ("core", "y", "x")
LINE = ("zh", "zl")
ALL = ("zh", "zl", "core", "y", "x")
VMEM = pl.BlockSpec(memory_space=pltpu.VMEM)
PARAMS = pltpu.CompilerParams(vmem_limit_bytes=40 * 1024 * 1024)


def normalize(embed):
    values = embed.astype(jnp.float32)
    inverse = lax.rsqrt(jnp.sum(values * values, axis=-1, keepdims=True) + 1e-06)
    return (values * inverse).astype(jnp.bfloat16)


def inner_of(left, right):
    return lax.dot_general(
        left, right, (((1,), (1,)), ((), ())), preferred_element_type=jnp.float32
    )


def log_total(parts):
    top = jnp.max(parts, axis=0)
    return top + jnp.log2(jnp.sum(jnp.exp2(parts - top[None]), axis=0))


def spread_rows(vector, column_ref):
    for block in range(vector.shape[0]):
        wide = jnp.broadcast_to(vector[block : block + 1], (LANES, LANES))
        column_ref[block * LANES : (block + 1) * LANES] = wide.T


def prepare_kernel(demo_ref, rollout_ref, demo_out, rollout_out):
    demo = normalize(demo_ref[...])
    for peer in range(demo_out.shape[0]):
        demo_out[peer] = demo
    rollout = normalize(rollout_ref[...])
    for peer in range(rollout_out.shape[0]):
        rollout_out[peer] = rollout


def row_lse_kernel(
    d0, d1, d2, d3, r0, r1, demo_ref, rollout_ref, out_ref, inner_ref, top_ref
):
    zl = lax.axis_index("zl")
    core = lax.axis_index("core")
    step = d0.shape[0]
    for turn, block in enumerate((d0, d1, d2, d3)):
        at = pl.multiple_of(lax.rem(zl + turn, 4) * step, step)
        demo_ref[pl.ds(at, step)] = block[...]
    half = r0.shape[0]
    rollout_ref[pl.ds(pl.multiple_of(core * half, half), half)] = r0[...]
    rollout_ref[pl.ds(pl.multiple_of((1 - core) * half, half), half)] = r1[...]
    rows = demo_ref.shape[0]
    chunks = rollout_ref.shape[0] // CHUNK
    top_ref[...] = jnp.full_like(top_ref, -4.0)

    def multiply(c, _):
        at = pl.multiple_of(c * CHUNK, CHUNK)
        inner = inner_of(demo_ref[...], rollout_ref[pl.ds(at, CHUNK)])
        inner_ref[c] = inner
        top_ref[...] = jnp.maximum(
            top_ref[...], jnp.maximum(inner[:, :LANES], inner[:, LANES:])
        )
        return 0

    lax.fori_loop(0, chunks, multiply, 0)

    def add_up(b, _):
        at = pl.ds(pl.multiple_of(b * LANES, LANES), LANES)
        top = top_ref[at]
        total = jnp.zeros_like(top)
        for c in range(chunks):
            for lane in (0, LANES):
                entry = inner_ref[c, at, lane : lane + LANES]
                total = total + jnp.exp2((entry - top) * SCALE)
        top, total = top.T, total.T
        peak = jnp.max(top, axis=0, keepdims=True)
        total = jnp.sum(total * jnp.exp2((top - peak) * SCALE), axis=0, keepdims=True)
        line = (peak - 1.0) * SCALE + jnp.log2(total)
        out_ref[:, pl.ds(b, 1)] = jnp.broadcast_to(line[None], (out_ref.shape[0], 1, LANES))
        return 0

    lax.fori_loop(0, rows // LANES, add_up, 0)


def col_lse_kernel(
    log_rows, parts_ref, demo_ref, rollout_ref, phi_ref, out_ref, column_ref, expo_ref, line_ref
):
    phi = -log_rows - log_total(parts_ref[...])
    phi_ref[...] = phi
    spread_rows(phi - SCALE, column_ref)
    rows = demo_ref.shape[0]

    def chunk(c, _):
        at = pl.multiple_of(c * CHUNK, CHUNK)
        inner = inner_of(demo_ref[...], rollout_ref[pl.ds(at, CHUNK)])
        for half in (0, 1):
            expo = inner[:, half * LANES : (half + 1) * LANES] * SCALE + column_ref[...]
            expo_ref[half] = expo
            top = jnp.max(expo.reshape(rows // 8, 8, LANES), axis=0)
            peak = jnp.max(top, axis=0, keepdims=True)
            total = jnp.sum(jnp.exp2(expo_ref[half] - peak), axis=0, keepdims=True)
            line_ref[pl.ds(2 * c + half, 1)] = peak + jnp.log2(total)
        return 0

    lax.fori_loop(0, rollout_ref.shape[0] // CHUNK, chunk, 0)
    out_ref[...] = jnp.broadcast_to(line_ref[...][None], out_ref.shape)


def row_sum_kernel(
    log_cols, parts_ref, phi_ref, demo_ref, rollout_ref, gamma_ref, out_ref, column_ref, total_ref
):
    gamma_ref[...] = -log_cols - log_total(parts_ref[...])
    spread_rows(phi_ref[...] - SCALE, column_ref)
    total_ref[...] = jnp.zeros_like(total_ref)

    def chunk(c, _):
        at = pl.multiple_of(c * CHUNK, CHUNK)
        inner = inner_of(demo_ref[...], rollout_ref[pl.ds(at, CHUNK)])
        column = column_ref[...]
        left = inner[:, :LANES] * SCALE + column + gamma_ref[pl.ds(2 * c, 1)]
        right = inner[:, LANES:] * SCALE + column + gamma_ref[pl.ds(2 * c + 1, 1)]
        total_ref[...] += jnp.exp2(left) + jnp.exp2(right)
        return 0

    lax.fori_loop(0, rollout_ref.shape[0] // CHUNK, chunk, 0)
    for block in range(out_ref.shape[1]):
        total = total_ref[block * LANES : (block + 1) * LANES].T
        line = jnp.sum(total, axis=0, keepdims=True)
        out_ref[:, block : block + 1] = jnp.broadcast_to(
            line[None], (out_ref.shape[0], 1, LANES)
        )


def col_sum_kernel(
    log_rows, parts_ref, phi_ref, gamma_ref, demo_ref, rollout_ref, phi_out, out_ref, column_ref,
    plan_ref, cost_ref
):
    phi = phi_ref[...] - log_rows - jnp.log2(jnp.sum(parts_ref[...], axis=0))
    phi_out[...] = phi
    spread_rows(phi - SCALE, column_ref)

    def chunk(c, _):
        at = pl.multiple_of(c * CHUNK, CHUNK)
        inner = inner_of(demo_ref[...], rollout_ref[pl.ds(at, CHUNK)])
        for half in (0, 1):
            entry = inner[:, half * LANES : (half + 1) * LANES]
            line = pl.ds(2 * c + half, 1)
            plan = jnp.exp2(entry * SCALE + column_ref[...] + gamma_ref[line])
            plan_ref[line] = jnp.sum(plan, axis=0, keepdims=True)
            cost_ref[line] = jnp.sum(plan * (1.0 - entry), axis=0, keepdims=True)
        return 0

    lax.fori_loop(0, rollout_ref.shape[0] // CHUNK, chunk, 0)
    share = LANES // 2
    low = lax.broadcasted_iota(jnp.int32, plan_ref.shape, 1) < share
    plan, cost = plan_ref[...], cost_ref[...]
    even = jnp.where(low, plan, pltpu.roll(cost, share, 1))
    odd = jnp.where(low, pltpu.roll(plan, share, 1), cost)
    for line in range(plan.shape[0]):
        out_ref[2 * line] = even[line : line + 1]
        out_ref[2 * line + 1] = odd[line : line + 1]


def call(kernel, outs, scratch, *args):
    return pl.pallas_call(
        kernel,
        out_shape=outs,
        in_specs=[VMEM] * len(args),
        out_specs=jax.tree.map(lambda _: VMEM, outs),
        scratch_shapes=scratch,
        compiler_params=PARAMS,
    )(*args)


def body(demo, rollout):
    f32, bf16 = jnp.float32, jnp.bfloat16
    shape = jax.ShapeDtypeStruct
    share, width = demo.shape
    n_zh, n_line, n_sheet = lax.axis_size("zh"), lax.axis_size(LINE), lax.axis_size(SHEET)
    n_plane = lax.axis_size(PLANE)
    rows, cols = share * n_line, share * n_sheet
    log_rows, log_cols = math.log2(rows * n_sheet), math.log2(cols * n_line)
    row_vec, col_vec = (rows // LANES, LANES), (cols // LANES, LANES)

    demo_send, rollout_send = call(
        prepare_kernel,
        (shape((n_zh, share, width), bf16), shape((n_plane, share, width), bf16)),
        [],
        demo,
        rollout,
    )
    near = lax.all_to_all(demo_send, "zh", 0, 0, tiled=True).reshape(n_zh * share, width)
    near, rollout_send = lax.optimization_barrier((near, rollout_send))
    n_z = n_line
    blocks = [near]
    for turn in (1, 2, -1):
        blocks.append(lax.ppermute(near, LINE, [((i + turn) % n_z, i) for i in range(n_z)]))
    mine = lax.all_to_all(rollout_send, PLANE, 0, 0, tiled=True).reshape(n_plane * share, width)
    other = lax.ppermute(mine, "core", [(0, 1), (1, 0)])

    demo_unit, rollout_unit, row_parts = call(
        row_lse_kernel,
        (
            shape((rows, width), bf16),
            shape((cols, width), bf16),
            shape((n_line,) + row_vec, f32),
        ),
        [pltpu.VMEM((cols // CHUNK, rows, CHUNK), f32), pltpu.VMEM((rows, LANES), f32)],
        *blocks,
        mine,
        other,
    )
    row_parts = lax.all_to_all(row_parts, LINE, 0, 0, tiled=True)
    phi, col_parts = call(
        functools.partial(col_lse_kernel, log_rows),
        (shape(row_vec, f32), shape((n_sheet,) + col_vec, f32)),
        [pltpu.VMEM((rows, LANES), f32), pltpu.VMEM((2, rows, LANES), f32), pltpu.VMEM(col_vec, f32)],
        row_parts,
        demo_unit,
        rollout_unit,
    )
    col_parts = lax.all_to_all(col_parts, SHEET, 0, 0, tiled=True)
    gamma, row_parts = call(
        functools.partial(row_sum_kernel, log_cols),
        (shape(col_vec, f32), shape((n_line,) + row_vec, f32)),
        [pltpu.VMEM((rows, LANES), f32), pltpu.VMEM((rows, LANES), f32)],
        col_parts,
        phi,
        demo_unit,
        rollout_unit,
    )
    row_parts = lax.all_to_all(row_parts, LINE, 0, 0, tiled=True)
    phi, sums = call(
        functools.partial(col_sum_kernel, log_rows),
        (shape(row_vec, f32), shape((n_sheet, 1, 2 * share), f32)),
        [pltpu.VMEM((rows, LANES), f32), pltpu.VMEM(col_vec, f32), pltpu.VMEM(col_vec, f32)],
        row_parts,
        phi,
        gamma,
        demo_unit,
        rollout_unit,
    )
    sums = lax.all_to_all(sums, SHEET, 0, 0, tiled=True)
    sums = jnp.sum(sums, axis=(0, 1))
    plan, cost = sums[:share], sums[share:]
    at = lax.axis_index(SHEET) * share
    gamma = lax.dynamic_slice_in_dim(gamma.reshape(-1), at, share)
    gamma = gamma - log_cols - jnp.log2(plan)
    reward = -cost / plan
    at = (lax.axis_index("zl") * n_zh + lax.axis_index("zh")) * share
    phi = lax.dynamic_slice_in_dim(phi.reshape(-1), at, share)
    return (phi * LN2, gamma * LN2, reward)


def solution(mesh):
    fine = Mesh(mesh.devices.reshape(4, 4, 2, 4, 4), ALL)
    return jax.shard_map(
        body,
        mesh=fine,
        in_specs=(P(ALL, None), P(ALL, None)),
        out_specs=(P(ALL), P(ALL), P(ALL)),
        check_vma=False,
    )
```

time: 521 us -> 146 us (0.28)
  blocking collectives: 402 us -> 76.2 us
  other arithmetic: 42.5 us -> 1.24 us
  waiting for transfers between devices: 55.3 us -> 22.2 us
  starting transfers between devices: 0.04 us -> 25.4 us
  Pallas kernels: 0 us -> 18.5 us
  between operations: 14.2 us -> 0.73 us
  matrix products: 5.74 us -> 0 us
    psum x5 -> x0, blocking collectives: 198 us -> none  [the longest x2 93.6 us: over_rows(): total = lax.psum(jnp.sum(jnp.exp(expo - top[None, :]), axis=0), 'row')]
    pmax x4 -> x0, blocking collectives: 185 us -> none  [the longest x2 121 us: over_rows(): top = lax.pmax(top, 'row')]
    all_to_all x0 -> x4, blocking collectives: none -> 76.2 us  [the longest x1 28.1 us: body(): lax.all_to_all(demo_send, 'zh', 0, 0, tiled=True)]
    all_gather x1 -> x0, waiting for transfers between devices: 55.2 us -> none  [body(): rollout_unit = lax.all_gather(normalize(rollout), 'row', axis=0, tiled=True)]
    reduce_sum x7 -> x1, other arithmetic: 25.4 us -> 0.05 us  [body(): sums = jnp.sum(sums, axis=(0, 1))]
    all_gather x1 -> x0, blocking collectives: 20 us -> none  [body(): demo_unit = lax.all_gather(normalize(demo), 'col', axis=0, tiled=True)]
    pallas_call x0 -> x5, Pallas kernels: none -> 18.5 us  [call(): pl.pallas_call(kernel, out_shape=outs, in_specs=[VMEM] * len(args), out_s...]
    all_to_all x0 -> x2, waiting for transfers between devices: none -> 17.7 us  [the longest x1 11.6 us: body(): row_parts = lax.all_to_all(row_parts, LINE, 0, 0, tiled=True)]
  transfers between devices with their start and end apart: 1 -> 6, of which waited for: 1 -> 4; matrix products, arithmetic and copies ran while one was open for 0% -> 0% of each run, Pallas kernels for 0% -> 0%
where the time goes in v1:
time: 146 us
  blocking collectives  76.2 us (52%)
  starting transfers between devices  25.4 us (17%)
  waiting for transfers between devices  22.2 us (15%)
  Pallas kernels  18.5 us (13%)
  local copies, waits for them, and re-layouts  1.51 us (1%)
    all_to_all x1, blocking collectives, body(): lax.all_to_all(demo_send, 'zh', 0, 0, tiled=True)  28.1 us
    pallas_call x5, Pallas kernels, call(): pl.pallas_call(kernel, out_shape=outs, in_specs=[VMEM] * len(args), out_s...  18.5 us
    all_to_all x1, blocking collectives, body(): row_parts = lax.all_to_all(row_parts, LINE, 0, 0, tiled=True)  18.2 us
    all_to_all x1, blocking collectives, body(): lax.all_to_all(rollout_send, PLANE, 0, 0, tiled=True)  15.5 us
    all_to_all x1, blocking collectives, body(): col_parts = lax.all_to_all(col_parts, SHEET, 0, 0, tiled=True)  14.3 us
    all_to_all x1, waiting for transfers between devices, body(): row_parts = lax.all_to_all(row_parts, LINE, 0, 0, tiled=True)  11.6 us
    ppermute x3, starting transfers between devices, body(): lax.ppermute(near, LINE, [((i + turn) % n_z, i) for i in range(n_z)])  9.85 us
    all_to_all x1, waiting for transfers between devices, body(): sums = lax.all_to_all(sums, SHEET, 0, 0, tiled=True)  6.11 us
  transfers between devices with their start and end apart: 6, of which 4 were waited for; matrix products, arithmetic and copies ran while one was open for 0% of the time, Pallas kernels for 0%

profile of v1, /device:TPU:1, one launch (start us, length us, event | category | flops | bytes accessed | tf_op | source)
XLA Modules:
  0.0 145.9 jit_solution(16698759161992361236)
XLA Ops:
  0.6 0.0 copy-start
  0.6 0.7 copy-done
  1.4 0.0 copy-start.1
  1.4 0.8 copy-done.1
  2.1 0.1 shard_map.49
  2.3 28.1 %all_to_all.30 = bf16[4,64,256]{2,1,0:T(8,128)(2,1)S(1)} all-to-all(bf16[4,64,256]{2,1,0:T(8,128)(2,1)S(1)} %get-tuple-element.16), channel_id=1, replica_groups=mesh['zh'=4,'zl'=4,'core'=2,'y'=4,'x'=4] {'zh'}, dimensions={0} | all-to-all | bytes 262144 | tf_op jit(solution)/shard_map/all_to_all | solution.py:209
  30.4 15.5 %all_to_all.31 = bf16[16,64,256]{2,1,0:T(8,128)(2,1)S(1)} all-to-all(bf16[16,64,256]{2,1,0:T(8,128)(2,1)S(1)} %get-tuple-element.19), channel_id=1, replica_groups=mesh['zh'=4,'zl'=4,'core'=2,'y'=4,'x'=4] {'y','x'}, dimensions={0} | all-to-all | bytes 1048576 | tf_op jit(solution)/shard_map/all_to_all | solution.py:215
  45.9 6.1 %collective-permute-start.3 = (bf16[1024,256]{1,0:T(8,128)(2,1)S(1)}, bf16[1024,256]{1,0:T(8,128)(2,1)S(1)}, u32[]{:S(2)}, u32[]{:S(2)}) collective-permute-start(bf16[1024,256]{1,0:T(8,128)(2,1)S(1)} %bitcast.4), channel_id=1, source_target_pairs={{0,16},{16,0},{1,17},{17,1},{2,18},{18,2},{3,19},{19,3},{4,20},{20... | collective-permute-start | bytes 1572872 | tf_op jit(solution)/shard_map/ppermute | solution.py:216
  52.0 2.8 %collective-permute-start = (bf16[256,256]{1,0:T(8,128)(2,1)S(1)}, bf16[256,256]{1,0:T(8,128)(2,1)S(1)}, u32[]{:S(2)}, u32[]{:S(2)}) collective-permute-start(bf16[256,256]{1,0:T(8,128)(2,1)S(1)} %bitcast.6), channel_id=1, source_target_pairs={{32,0},{64,32},{96,64},{128,96},{160,128},{192,160},{224,192},{256... | collective-permute-start | bytes 393224 | tf_op jit(solution)/shard_map/ppermute | solution.py:214
  54.8 3.7 %collective-permute-start.1 = (bf16[256,256]{1,0:T(8,128)(2,1)S(1)}, bf16[256,256]{1,0:T(8,128)(2,1)S(1)}, u32[]{:S(2)}, u32[]{:S(2)}) collective-permute-start(bf16[256,256]{1,0:T(8,128)(2,1)S(1)} %bitcast.7), channel_id=1, source_target_pairs={{64,0},{96,32},{128,64},{160,96},{192,128},{224,160},{256,192},{28... | collective-permute-start | bytes 393224 | tf_op jit(solution)/shard_map/ppermute | solution.py:214
  58.5 3.4 %collective-permute-start.2 = (bf16[256,256]{1,0:T(8,128)(2,1)S(1)}, bf16[256,256]{1,0:T(8,128)(2,1)S(1)}, u32[]{:S(2)}, u32[]{:S(2)}) collective-permute-start(bf16[256,256]{1,0:T(8,128)(2,1)S(1)} %bitcast.8), channel_id=1, source_target_pairs={{480,0},{0,32},{32,64},{64,96},{96,128},{128,160},{160,192},{192,2... | collective-permute-start | bytes 393224 | tf_op jit(solution)/shard_map/ppermute | solution.py:214
  61.9 0.0 collective-permute-done.d1
  61.9 3.7 %collective-permute-done.1.d2 = bf16[256,256]{1,0:T(8,128)(2,1)S(1)} collective-permute-done((bf16[256,256]{1,0:T(8,128)(2,1)S(1)}, bf16[256,256]{1,0:T(8,128)(2,1)S(1)}, u32[]{:S(2)}, u32[]{:S(2)}) %collective-permute-start.1) | collective-permute-done | bytes 131104 | tf_op jit(solution)/shard_map/ppermute | solution.py:214
  65.6 0.8 collective-permute-done.2.d3
  66.4 0.0 collective-permute-done.3.r1
  66.4 4.7 %shard_map.50 = (bf16[1024,256]{1,0:T(8,128)(2,1)S(1)}, bf16[2048,256]{1,0:T(8,128)(2,1)S(1)}, f32[16,8,128]{2,1,0:T(8,128)S(1)}) custom-call(bf16[256,256]{1,0:T(8,128)(2,1)S(1)} %bitcast.9, bf16[256,256]{1,0:T(8,128)(2,1)S(1)} %collective-permute-done.d1, bf16[256,256]{1,0:T(8,128)(2,1)S(1)} %collective-permute-done.1.d2, ...), custom_call_target="tpu_custom_call" | custom-call | tf_op jit(solution)/shard_map/pallas_call | solution.py:182
  71.1 18.2 %all_to_all.32.parts_ref = f32[16,8,128]{2,1,0:T(8,128)S(1)} all-to-all(f32[16,8,128]{2,1,0:T(8,128)S(1)} %get-tuple-element.20), channel_id=1, replica_groups=mesh['zh'=4,'zl'=4,'core'=2,'y'=4,'x'=4] {'zh','zl'}, dimensions={0} | all-to-all | bytes 131072 | tf_op jit(solution)/shard_map/all_to_all | solution.py:230
  89.4 4.8 %shard_map.51 = (f32[8,128]{1,0:T(8,128)S(1)}, f32[32,16,128]{2,1,0:T(8,128)S(1)}) custom-call(f32[16,8,128]{2,1,0:T(8,128)S(1)} %all_to_all.32.parts_ref, bf16[1024,256]{1,0:T(8,128)(2,1)S(1)} %get-tuple-element.21.demo_ref, bf16[2048,256]{1,0:T(8,128)(2,1)S(1)} %get-tuple-element.22.rollout_ref), custom_call_target="tpu_custom_call" | custom-call | tf_op jit(solution)/shard_map/pallas_call | solution.py:182
  94.2 14.3 %all_to_all.33.parts_ref = f32[32,16,128]{2,1,0:T(8,128)S(1)} all-to-all(f32[32,16,128]{2,1,0:T(8,128)S(1)} %get-tuple-element.23), channel_id=1, replica_groups=mesh['zh'=4,'zl'=4,'core'=2,'y'=4,'x'=4] {'core','y','x'}, dimensions={0} | all-to-all | bytes 524288 | tf_op jit(solution)/shard_map/all_to_all | solution.py:239
  108.5 4.0 %shard_map.52 = (f32[16,128]{1,0:T(8,128)S(1)}, f32[16,8,128]{2,1,0:T(8,128)}) custom-call(f32[32,16,128]{2,1,0:T(8,128)S(1)} %all_to_all.33.parts_ref, f32[8,128]{1,0:T(8,128)S(1)} %get-tuple-element.24.phi_ref, bf16[1024,256]{1,0:T(8,128)(2,1)S(1)} %get-tuple-element.21.demo_ref, bf16[2048,256]{1,0:T(8,128)(2,1)S(1)} %get-tuple-element.22.rollout_ref), custom_call_target="tpu_custom_call" | custom-call | tf_op jit(solution)/shard_map/pallas_call | solution.py:182
  112.6 3.5 %all-to-all-start.4 = ((f32[16,8,128]{2,1,0:T(8,128)}), f32[16,8,128]{2,1,0:T(8,128)S(1)}, u32[]{:S(2)}, u32[]{:S(2)}) async-start(f32[16,8,128]{2,1,0:T(8,128)} %get-tuple-element.25), calls=%async_computation.4 | async-start | bytes 131072 | tf_op jit(solution)/shard_map/all_to_all | solution.py:249
  116.1 11.6 %all-to-all-done.4.parts_ref = f32[16,8,128]{2,1,0:T(8,128)S(1)} async-done(((f32[16,8,128]{2,1,0:T(8,128)}), f32[16,8,128]{2,1,0:T(8,128)S(1)}, u32[]{:S(2)}, u32[]{:S(2)}) %all-to-all-start.4) | async-done | bytes 65568 | tf_op jit(solution)/shard_map/all_to_all | solution.py:249
  127.7 4.8 %shard_map.53 = (f32[8,128]{1,0:T(8,128)S(1)}, f32[32,1,128]{2,1,0:T(1,128)}) custom-call(f32[16,8,128]{2,1,0:T(8,128)S(1)} %all-to-all-done.4.parts_ref, f32[8,128]{1,0:T(8,128)S(1)} %get-tuple-element.24.phi_ref, f32[16,128]{1,0:T(8,128)S(1)} %get-tuple-element.26.gamma_ref, bf16[1024,256]{1,0:T(8,128)(2,1)S(1)} %get-tuple-element.21.demo_ref, ...), custom_call_target="tpu_custom_call" | custom-call | tf_op jit(solution)/shard_map/pallas_call | solution.py:182
  132.5 6.0 %all-to-all-start.5 = ((f32[32,1,128]{2,1,0:T(1,128)}), f32[32,1,128]{2,1,0:T(1,128)S(1)}, u32[]{:S(2)}, u32[]{:S(2)}) async-start(f32[32,1,128]{2,1,0:T(1,128)} %get-tuple-element.28), calls=%async_computation.5 | async-start | bytes 32768 | tf_op jit(solution)/shard_map/all_to_all | solution.py:260
  138.5 0.6 dynamic-slice_multiply_fusion
  139.1 6.1 %all-to-all-done.5 = f32[32,1,128]{2,1,0:T(1,128)S(1)} async-done(((f32[32,1,128]{2,1,0:T(1,128)}), f32[32,1,128]{2,1,0:T(1,128)S(1)}, u32[]{:S(2)}, u32[]{:S(2)}) %all-to-all-start.5) | async-done | bytes 16416 | tf_op jit(solution)/shard_map/all_to_all | solution.py:260
  145.2 0.1 reduce_sum.9
  145.3 0.6 negate_divide_fusion
Async XLA Ops:
  0.6 0.8 copy-start
  1.4 0.8 copy-start.1
  45.9 20.5 %collective-permute-start.3 = (bf16[1024,256]{1,0:T(8,128)(2,1)S(1)}, bf16[1024,256]{1,0:T(8,128)(2,1)S(1)}, u32[]{:S(2)}, u32[]{:S(2)}) collective-permute-start(bf16[1024,256]{1,0:T(8,128)(2,1)S(1)} %bitcast.4), channel_id=1, source_target_pairs={{0,16},{16,0},{1,17},{17,1},{2,18},{18,2},{3,19},{19,3},{4,20},{20... | collective-permute-start | bytes 1572872 | tf_op jit(solution)/shard_map/ppermute | solution.py:216
  52.0 9.9 %collective-permute-start = (bf16[256,256]{1,0:T(8,128)(2,1)S(1)}, bf16[256,256]{1,0:T(8,128)(2,1)S(1)}, u32[]{:S(2)}, u32[]{:S(2)}) collective-permute-start(bf16[256,256]{1,0:T(8,128)(2,1)S(1)} %bitcast.6), channel_id=1, source_target_pairs={{32,0},{64,32},{96,64},{128,96},{160,128},{192,160},{224,192},{256... | collective-permute-start | bytes 393224 | tf_op jit(solution)/shard_map/ppermute | solution.py:214
  54.8 10.8 %collective-permute-start.1 = (bf16[256,256]{1,0:T(8,128)(2,1)S(1)}, bf16[256,256]{1,0:T(8,128)(2,1)S(1)}, u32[]{:S(2)}, u32[]{:S(2)}) collective-permute-start(bf16[256,256]{1,0:T(8,128)(2,1)S(1)} %bitcast.7), channel_id=1, source_target_pairs={{64,0},{96,32},{128,64},{160,96},{192,128},{224,160},{256,192},{28... | collective-permute-start | bytes 393224 | tf_op jit(solution)/shard_map/ppermute | solution.py:214
  58.5 7.9 %collective-permute-start.2 = (bf16[256,256]{1,0:T(8,128)(2,1)S(1)}, bf16[256,256]{1,0:T(8,128)(2,1)S(1)}, u32[]{:S(2)}, u32[]{:S(2)}) collective-permute-start(bf16[256,256]{1,0:T(8,128)(2,1)S(1)} %bitcast.8), channel_id=1, source_target_pairs={{480,0},{0,32},{32,64},{64,96},{96,128},{128,160},{160,192},{192,2... | collective-permute-start | bytes 393224 | tf_op jit(solution)/shard_map/ppermute | solution.py:214
  112.6 15.1 %all-to-all-start.4 = ((f32[16,8,128]{2,1,0:T(8,128)}), f32[16,8,128]{2,1,0:T(8,128)S(1)}, u32[]{:S(2)}, u32[]{:S(2)}) async-start(f32[16,8,128]{2,1,0:T(8,128)} %get-tuple-element.25), calls=%async_computation.4 | async-start | bytes 131072 | tf_op jit(solution)/shard_map/all_to_all | solution.py:249
  132.5 12.8 %all-to-all-start.5 = ((f32[32,1,128]{2,1,0:T(1,128)}), f32[32,1,128]{2,1,0:T(1,128)S(1)}, u32[]{:S(2)}, u32[]{:S(2)}) async-start(f32[32,1,128]{2,1,0:T(1,128)} %get-tuple-element.28), calls=%async_computation.5 | async-start | bytes 32768 | tf_op jit(solution)/shard_map/all_to_all | solution.py:260

commit v2 on v0

v2 whole, which is shorter than its diff:
```python
import functools
import math

import jax
import jax.numpy as jnp
from jax import lax
from jax.experimental import pallas as pl
from jax.experimental.pallas import tpu as pltpu
from jax.sharding import Mesh
from jax.sharding import PartitionSpec as P

EPS = 0.005
SCALE = 1.0 / (EPS * math.log(2.0))
LN2 = math.log(2.0)
LANES = 128
CHUNK = 256
PLANE = ("y", "x")
SHEET = ("core", "y", "x")
LINE = ("zh", "zl")
ALL = ("zh", "zl", "core", "y", "x")
VMEM = pl.BlockSpec(memory_space=pltpu.VMEM)
PARAMS = pltpu.CompilerParams(vmem_limit_bytes=6 * 1024 * 1024)


def normalize(embed):
    values = embed.astype(jnp.float32)
    inverse = lax.rsqrt(jnp.sum(values * values, axis=-1, keepdims=True) + 1e-06)
    return (values * inverse).astype(jnp.bfloat16)


def inner_of(left, right):
    return lax.dot_general(
        left, right, (((1,), (1,)), ((), ())), preferred_element_type=jnp.float32
    )


def log_total(parts):
    top = jnp.max(parts, axis=0)
    return top + jnp.log2(jnp.sum(jnp.exp2(parts - top[None]), axis=0))


def spread_rows(vector, column_ref):
    for block in range(vector.shape[0]):
        wide = jnp.broadcast_to(vector[block : block + 1], (LANES, LANES))
        column_ref[block * LANES : (block + 1) * LANES] = wide.T


def block_of(index, size):
    return pl.ds(pl.multiple_of(index * size, size), size)


def prepare_kernel(in_ref, out_ref):
    unit = normalize(in_ref[...])
    for peer in range(out_ref.shape[0]):
        out_ref[peer] = unit


def row_lse_kernel(demo_ref, mine_ref, other_ref, inner_ref, out_ref, top_ref, total_ref):
    core = lax.axis_index("core")
    chunks, rows = inner_ref.shape[:2]
    half = chunks // 2
    top = None
    for side, ref in ((core, mine_ref), (1 - core, other_ref)):
        for c in range(half // 2):
            inner = inner_of(demo_ref[...], ref[c * CHUNK : (c + 1) * CHUNK]) * SCALE
            left, right = inner[:, :LANES], inner[:, LANES:]
            inner_ref[side * half + 2 * c] = left
            inner_ref[side * half + 2 * c + 1] = right
            peak = jnp.maximum(left, right)
            top_ref[...] = peak if top is None else jnp.maximum(top_ref[...], peak)
            top = True

    def add_up(b, _):
        at = block_of(b, 64)
        top = top_ref[at]
        total = jnp.zeros_like(top)
        for c in range(chunks):
            total = total + jnp.exp2(inner_ref[c, at] - top)
        total_ref[at] = total
        return 0

    lax.fori_loop(0, rows // 64, add_up, 0)
    for block in range(rows // LANES):
        at = slice(block * LANES, (block + 1) * LANES)
        top, total = top_ref[at].T, total_ref[at].T
        peak = jnp.max(top, axis=0, keepdims=True)
        total = jnp.sum(total * jnp.exp2(top - peak), axis=0, keepdims=True)
        line = peak - SCALE + jnp.log2(total)
        out_ref[:, block : block + 1] = jnp.broadcast_to(line[None], (out_ref.shape[0], 1, LANES))


def col_lse_kernel(
    log_rows, parts_ref, inner_ref, phi_ref, expo_ref, out_ref, column_ref, line_ref
):
    phi = -log_rows - log_total(parts_ref[...])
    phi_ref[...] = phi
    spread_rows(phi - SCALE, column_ref)
    chunks, rows = inner_ref.shape[:2]
    width = 4

    def group(g, _):
        tops = [None] * width
        for row in range(0, rows, 8):
            at = slice(row, row + 8)
            column = column_ref[at]
            for w in range(width):
                expo = inner_ref[g * width + w, at] + column
                expo_ref[g * width + w, at] = expo
                tops[w] = expo if row == 0 else jnp.maximum(tops[w], expo)
        totals = [jnp.zeros((8, LANES), jnp.float32)] * width
        for row in range(0, rows, 8):
            for w in range(width):
                expo = expo_ref[g * width + w, slice(row, row + 8)]
                totals[w] = totals[w] + jnp.exp2(expo - tops[w])
        for w in range(width):
            peak = jnp.max(tops[w], axis=0, keepdims=True)
            total = jnp.sum(totals[w] * jnp.exp2(tops[w] - peak), axis=0, keepdims=True)
            line_ref[pl.ds(g * width + w, 1)] = peak + jnp.log2(total)
        return 0

    lax.fori_loop(0, chunks // width, group, 0)
    out_ref[...] = jnp.broadcast_to(line_ref[...][None], out_ref.shape)


def row_sum_kernel(log_cols, parts_ref, expo_ref, gamma_ref, plan_ref, out_ref, total_ref):
    gamma = -log_cols - log_total(parts_ref[...])
    gamma_ref[...] = gamma
    chunks, rows = expo_ref.shape[:2]

    def add_up(b, _):
        at = block_of(b, LANES)
        total = jnp.zeros((LANES, LANES), jnp.float32)
        for c in range(chunks):
            plan = jnp.exp2(expo_ref[c, at] + gamma[c : c + 1])
            plan_ref[c, at] = plan
            total = total + plan
        total_ref[at] = total
        return 0

    lax.fori_loop(0, rows // LANES, add_up, 0)
    for block in range(rows // LANES):
        total = total_ref[block * LANES : (block + 1) * LANES].T
        line = jnp.sum(total, axis=0, keepdims=True)
        out_ref[:, block : block + 1] = jnp.broadcast_to(line[None], (out_ref.shape[0], 1, LANES))


def col_sum_kernel(
    log_rows, parts_ref, phi_ref, plan_ref, inner_ref, phi_out, out_ref, column_ref
):
    change = -log_rows - jnp.log2(jnp.sum(parts_ref[...], axis=0))
    phi_out[...] = phi_ref[...] + change
    spread_rows(jnp.exp2(change), column_ref)
    chunks, rows = plan_ref.shape[:2]
    step = 128

    def add_up(b, totals):
        totals = list(totals)
        for row in range(0, step, 8):
            at = pl.ds(pl.multiple_of(b * step + row, 8), 8)
            column = column_ref[at]
            for c in range(chunks):
                plan = plan_ref[c, at] * column
                totals[c] = totals[c] + plan
                totals[chunks + c] = totals[chunks + c] + plan * (SCALE - inner_ref[c, at])
        return tuple(totals)

    zero = jnp.zeros((8, LANES), jnp.float32)
    totals = lax.fori_loop(0, rows // step, add_up, (zero,) * (2 * chunks))
    share = LANES // 2
    low = lax.broadcasted_iota(jnp.int32, (1, LANES), 1) < share
    for c in range(chunks):
        plan = jnp.sum(totals[c], axis=0, keepdims=True)
        cost = jnp.sum(totals[chunks + c], axis=0, keepdims=True) * (1.0 / SCALE)
        out_ref[2 * c] = jnp.where(low, plan, pltpu.roll(cost, share, 1))
        out_ref[2 * c + 1] = jnp.where(low, pltpu.roll(plan, share, 1), cost)


def own_half(ref, index):
    line = ref[pl.ds(lax.div(index, 2), 1)]
    share = LANES // 2
    moved = pltpu.roll(line, share, 1)
    return jnp.where(lax.rem(index, 2) == 0, line, moved)[:, :share]


def finish_kernel(log_cols, ratio, sums_ref, phi_ref, gamma_ref, phi_out, gamma_out, reward_out):
    total = sums_ref[0]
    for peer in range(1, sums_ref.shape[0]):
        total = total + sums_ref[peer]
    share = LANES // 2
    plan, cost = total[:, :share], pltpu.roll(total, share, 1)[:, :share]
    phi_out[...] = own_half(phi_ref, lax.axis_index("zh") * 4 + lax.axis_index("zl")) * LN2
    spot = lax.axis_index("core") * 16 + lax.axis_index("y") * 4 + lax.axis_index("x")
    gamma_out[...] = (own_half(gamma_ref, spot) - log_cols - jnp.log2(plan)) * LN2
    reward_out[...] = -ratio * cost / plan


def call(kernel, outs, scratch, *args):
    return pl.pallas_call(
        kernel,
        out_shape=outs,
        in_specs=[VMEM] * len(args),
        out_specs=jax.tree.map(lambda _: VMEM, outs),
        scratch_shapes=scratch,
        compiler_params=PARAMS,
    )(*args)


def body(demo, rollout):
    f32, bf16 = jnp.float32, jnp.bfloat16
    shape = jax.ShapeDtypeStruct
    share, width = demo.shape
    n_zh, n_line, n_sheet = lax.axis_size("zh"), lax.axis_size(LINE), lax.axis_size(SHEET)
    rows, cols = share * n_line, share * n_sheet
    log_rows, log_cols = math.log2(rows * n_sheet), math.log2(cols * n_line)
    row_vec, col_vec = (rows // LANES, LANES), (cols // LANES, LANES)
    tile = shape((cols // LANES, rows, LANES), f32)
    column = pltpu.VMEM((rows, LANES), f32)

    demo_send = call(prepare_kernel, shape((n_line, share, width), bf16), [], demo)
    rollout_send = call(prepare_kernel, shape((1, share, width), bf16), [], rollout)
    demo_unit = lax.all_to_all(demo_send, LINE, 0, 0, tiled=True).reshape(rows, width)
    mine = lax.all_gather(rollout_send[0], PLANE, axis=0, tiled=True)
    other = lax.ppermute(mine, "core", [(0, 1), (1, 0)])

    inner, row_parts = call(
        row_lse_kernel,
        (tile, shape((n_line,) + row_vec, f32)),
        [column, column],
        demo_unit,
        mine,
        other,
    )
    row_parts = lax.all_to_all(row_parts, LINE, 0, 0, tiled=True)
    phi, expo, col_parts = call(
        functools.partial(col_lse_kernel, log_rows),
        (shape(row_vec, f32), tile, shape((n_sheet,) + col_vec, f32)),
        [column, pltpu.VMEM(col_vec, f32)],
        row_parts,
        inner,
    )
    col_parts = lax.all_to_all(col_parts, SHEET, 0, 0, tiled=True)
    gamma, plan, row_parts = call(
        functools.partial(row_sum_kernel, log_cols),
        (shape(col_vec, f32), tile, shape((n_line,) + row_vec, f32)),
        [column],
        col_parts,
        expo,
    )
    row_parts = lax.all_to_all(row_parts, LINE, 0, 0, tiled=True)
    phi, sums = call(
        functools.partial(col_sum_kernel, log_rows),
        (shape(row_vec, f32), shape((n_sheet, 1, 2 * share), f32)),
        [column],
        row_parts,
        phi,
        plan,
        inner,
    )
    sums = lax.all_to_all(sums, SHEET, 0, 0, tiled=True)
    outs = call(
        functools.partial(finish_kernel, log_cols, 2.0 ** (log_cols - log_rows)),
        (shape((1, share), f32),) * 3,
        [],
        sums,
        phi,
        gamma,
    )
    return tuple(out.reshape(share) for out in outs)


def solution(mesh):
    fine = Mesh(mesh.devices.reshape(4, 4, 2, 4, 4), ALL)
    return jax.shard_map(
        body,
        mesh=fine,
        in_specs=(P(ALL, None), P(ALL, None)),
        out_specs=(P(ALL), P(ALL), P(ALL)),
        check_vma=False,
    )
```

time: 521 us -> 123 us (0.24)
  blocking collectives: 402 us -> 84.8 us
  waiting for transfers between devices: 55.3 us -> 1.52 us
  other arithmetic: 42.5 us -> 0 us
  starting transfers between devices: 0.04 us -> 23.2 us
  between operations: 14.2 us -> 0.7 us
  Pallas kernels: 0 us -> 10.3 us
  matrix products: 5.74 us -> 0 us
    psum x5 -> x0, blocking collectives: 198 us -> none  [the longest x2 93.6 us: over_rows(): total = lax.psum(jnp.sum(jnp.exp(expo - top[None, :]), axis=0), 'row')]
    pmax x4 -> x0, blocking collectives: 185 us -> none  [the longest x2 121 us: over_rows(): top = lax.pmax(top, 'row')]
    all_to_all x0 -> x4, blocking collectives: none -> 64.8 us  [the longest x2 37.4 us: body(): row_parts = lax.all_to_all(row_parts, LINE, 0, 0, tiled=True)]
    all_gather x1 -> x0, waiting for transfers between devices: 55.2 us -> none  [body(): rollout_unit = lax.all_gather(normalize(rollout), 'row', axis=0, tiled=True)]
    reduce_sum x7 -> x0, other arithmetic: 25.4 us -> none  [the longest x2 9.26 us: over_rows(): total = lax.psum(jnp.sum(jnp.exp(expo - top[None, :]), axis=0), 'row')]
    all_to_all x0 -> x1, starting transfers between devices: none -> 15.7 us  [body(): lax.all_to_all(demo_send, LINE, 0, 0, tiled=True).reshape(rows, width)]
    reduce_max x3 -> x0, other arithmetic: 13.6 us -> none  [the longest x2 9.07 us: over_rows(): top = jnp.max(expo, axis=0)]
    pallas_call x0 -> x7, Pallas kernels: none -> 10.3 us  [call(): pl.pallas_call(kernel, out_shape=outs, in_specs=[VMEM] * len(args), out_s...]
  transfers between devices with their start and end apart: 1 -> 2, of which waited for: 1 -> 1; matrix products, arithmetic and copies ran while one was open for 0% -> 0% of each run, Pallas kernels for 0% -> 0%
where the time goes in v2:
time: 123 us; the launch traced here: 122 us
  blocking collectives  84.8 us (69%)
  starting transfers between devices  23.2 us (19%)
  Pallas kernels  10.3 us (8%)
  waiting for transfers between devices  1.52 us (1%)
  local copies, waits for them, and re-layouts  1.5 us (1%)
    all_to_all x2, blocking collectives, body(): row_parts = lax.all_to_all(row_parts, LINE, 0, 0, tiled=True)  37.4 us
    all_gather x1, blocking collectives, body(): mine = lax.all_gather(rollout_send[0], PLANE, axis=0, tiled=True)  20 us
    all_to_all x1, starting transfers between devices, body(): lax.all_to_all(demo_send, LINE, 0, 0, tiled=True).reshape(rows, width)  15.7 us
    all_to_all x1, blocking collectives, body(): col_parts = lax.all_to_all(col_parts, SHEET, 0, 0, tiled=True)  14.8 us
    all_to_all x1, blocking collectives, body(): sums = lax.all_to_all(sums, SHEET, 0, 0, tiled=True)  12.6 us
    pallas_call x7, Pallas kernels, call(): pl.pallas_call(kernel, out_shape=outs, in_specs=[VMEM] * len(args), out_s...  10.3 us
    ppermute x1, starting transfers between devices, body(): other = lax.ppermute(mine, 'core', [(0, 1), (1, 0)])  7.48 us
  transfers between devices with their start and end apart: 2, of which 1 were waited for; matrix products, arithmetic and copies ran while one was open for 0% of the time, Pallas kernels for 0%

profile of v2, /device:TPU:1, one launch (start us, length us, event | category | flops | bytes accessed | tf_op | source)
XLA Modules:
  0.0 122.0 jit_solution(2018691581785478364)
XLA Ops:
  0.6 0.0 copy-start
  0.6 0.7 copy-done
  1.4 0.9 shard_map.49
  2.3 15.7 %all-to-all-start = ((bf16[16,64,256]{2,1,0:T(8,128)(2,1)}), bf16[16,64,256]{2,1,0:T(8,128)(2,1)S(1)}, u32[]{:S(2)}, u32[]{:S(2)}) async-start(bf16[16,64,256]{2,1,0:T(8,128)(2,1)} %shard_map.49), calls=%async_computation | async-start | bytes 1048576 | tf_op jit(solution)/shard_map/all_to_all | solution.py:221
  18.1 0.0 copy-start.1
  18.1 0.7 copy-done.1
  18.8 0.1 shard_map.50
  18.9 20.0 %all-gather = bf16[1,1024,256]{2,1,0:T(8,128)(2,1)S(1)} all-gather(bf16[1,64,256]{2,1,0:T(8,128)(2,1)S(1)} %shard_map.50), channel_id=2, replica_groups=mesh['zh'=4,'zl'=4,'core'=2,'y'=4,'x'=4] {'y','x'}, dimensions={1}, use_global_device_ids=true | all-gather | bytes 557056 | tf_op jit(solution)/shard_map/all_gather | solution.py:222
  39.0 7.5 %collective-permute-start = (bf16[1024,256]{1,0:T(8,128)(2,1)S(1)}, bf16[1024,256]{1,0:T(8,128)(2,1)S(1)}, u32[]{:S(2)}, u32[]{:S(2)}) collective-permute-start(bf16[1024,256]{1,0:T(8,128)(2,1)S(1)} %bitcast.6), channel_id=1, source_target_pairs={{0,16},{16,0},{1,17},{17,1},{2,18},{18,2},{3,19},{19,3},{4,20},{20... | collective-permute-start | bytes 1572872 | tf_op jit(solution)/shard_map/ppermute | solution.py:223
  46.4 1.5 %collective-permute-done.other_ref = bf16[1024,256]{1,0:T(8,128)(2,1)S(1)} collective-permute-done((bf16[1024,256]{1,0:T(8,128)(2,1)S(1)}, bf16[1024,256]{1,0:T(8,128)(2,1)S(1)}, u32[]{:S(2)}, u32[]{:S(2)}) %collective-permute-start) | collective-permute-done | bytes 524320 | tf_op jit(solution)/shard_map/ppermute | solution.py:223
  48.0 0.0 all-to-all-done
  48.0 3.1 %shard_map.51 = (f32[16,1024,128]{2,1,0:T(8,128)S(1)}, f32[16,8,128]{2,1,0:T(8,128)S(1)}) custom-call(bf16[1024,256]{1,0:T(8,128)(2,1)S(1)} %bitcast.5, bf16[1024,256]{1,0:T(8,128)(2,1)S(1)} %bitcast.7, bf16[1024,256]{1,0:T(8,128)(2,1)S(1)} %collective-permute-done.other_ref), custom_call_target="tpu_custom_call" | custom-call | tf_op jit(solution)/shard_map/pallas_call | solution.py:198
  51.0 23.2 %all_to_all.25.parts_ref = f32[16,8,128]{2,1,0:T(8,128)S(1)} all-to-all(f32[16,8,128]{2,1,0:T(8,128)S(1)} %get-tuple-element.16), channel_id=1, replica_groups=mesh['zh'=4,'zl'=4,'core'=2,'y'=4,'x'=4] {'zh','zl'}, dimensions={0} | all-to-all | bytes 131072 | tf_op jit(solution)/shard_map/all_to_all | solution.py:233
  74.2 2.2 %shard_map.52 = (f32[8,128]{1,0:T(8,128)S(1)}, f32[16,1024,128]{2,1,0:T(8,128)S(1)}, f32[32,16,128]{2,1,0:T(8,128)S(1)}) custom-call(f32[16,8,128]{2,1,0:T(8,128)S(1)} %all_to_all.25.parts_ref, f32[16,1024,128]{2,1,0:T(8,128)S(1)} %get-tuple-element.17.inner_ref), custom_call_target="tpu_custom_call" | custom-call | tf_op jit(solution)/shard_map/pallas_call | solution.py:198
  76.4 14.8 %all_to_all.26.parts_ref = f32[32,16,128]{2,1,0:T(8,128)S(1)} all-to-all(f32[32,16,128]{2,1,0:T(8,128)S(1)} %get-tuple-element.18), channel_id=1, replica_groups=mesh['zh'=4,'zl'=4,'core'=2,'y'=4,'x'=4] {'core','y','x'}, dimensions={0} | all-to-all | bytes 524288 | tf_op jit(solution)/shard_map/all_to_all | solution.py:241
  91.2 1.5 %shard_map.53 = (f32[16,128]{1,0:T(8,128)S(1)}, f32[16,1024,128]{2,1,0:T(8,128)S(1)}, f32[16,8,128]{2,1,0:T(8,128)S(1)}) custom-call(f32[32,16,128]{2,1,0:T(8,128)S(1)} %all_to_all.26.parts_ref, f32[16,1024,128]{2,1,0:T(8,128)S(1)} %get-tuple-element.19.expo_ref), custom_call_target="tpu_custom_call" | custom-call | tf_op jit(solution)/shard_map/pallas_call | solution.py:198
  92.7 14.2 %all_to_all.27.parts_ref = f32[16,8,128]{2,1,0:T(8,128)S(1)} all-to-all(f32[16,8,128]{2,1,0:T(8,128)S(1)} %get-tuple-element.20), channel_id=1, replica_groups=mesh['zh'=4,'zl'=4,'core'=2,'y'=4,'x'=4] {'zh','zl'}, dimensions={0} | all-to-all | bytes 131072 | tf_op jit(solution)/shard_map/all_to_all | solution.py:249
  106.9 1.9 %shard_map.54 = (f32[8,128]{1,0:T(8,128)S(1)}, f32[32,1,128]{2,1,0:T(1,128)S(1)}) custom-call(f32[16,8,128]{2,1,0:T(8,128)S(1)} %all_to_all.27.parts_ref, f32[8,128]{1,0:T(8,128)S(1)} %get-tuple-element.21.phi_ref, f32[16,1024,128]{2,1,0:T(8,128)S(1)} %get-tuple-element.22.plan_ref, f32[16,1024,128]{2,1,0:T(8,128)S(1)} %get-tuple-element.17.inner_ref), custom_call_target="tpu_custom_call" | custom-call | tf_op jit(solution)/shard_map/pallas_call | solution.py:198
  108.8 12.6 %all_to_all.28.sums_ref = f32[32,1,128]{2,1,0:T(1,128)S(1)} all-to-all(f32[32,1,128]{2,1,0:T(1,128)S(1)} %get-tuple-element.23), channel_id=1, replica_groups=mesh['zh'=4,'zl'=4,'core'=2,'y'=4,'x'=4] {'core','y','x'}, dimensions={0} | all-to-all | bytes 32768 | tf_op jit(solution)/shard_map/all_to_all | solution.py:259
  121.4 0.6 shard_map.55
Async XLA Ops:
  0.6 0.8 copy-start
  2.3 45.6 %all-to-all-start = ((bf16[16,64,256]{2,1,0:T(8,128)(2,1)}), bf16[16,64,256]{2,1,0:T(8,128)(2,1)S(1)}, u32[]{:S(2)}, u32[]{:S(2)}) async-start(bf16[16,64,256]{2,1,0:T(8,128)(2,1)} %shard_map.49), calls=%async_computation | async-start | bytes 1048576 | tf_op jit(solution)/shard_map/all_to_all | solution.py:221
  18.1 0.8 copy-start.1
  39.0 9.0 %collective-permute-start = (bf16[1024,256]{1,0:T(8,128)(2,1)S(1)}, bf16[1024,256]{1,0:T(8,128)(2,1)S(1)}, u32[]{:S(2)}, u32[]{:S(2)}) collective-permute-start(bf16[1024,256]{1,0:T(8,128)(2,1)S(1)} %bitcast.6), channel_id=1, source_target_pairs={{0,16},{16,0},{1,17},{17,1},{2,18},{18,2},{3,19},{19,3},{4,20},{20... | collective-permute-start | bytes 1572872 | tf_op jit(solution)/shard_map/ppermute | solution.py:223

commit v3 on v2

--- a/solution.py
+++ b/solution.py
@@ -45,41 +45,31 @@
         column_ref[block * LANES : (block + 1) * LANES] = wide.T
 
 
-def block_of(index, size):
-    return pl.ds(pl.multiple_of(index * size, size), size)
-
-
-def prepare_kernel(in_ref, out_ref):
-    unit = normalize(in_ref[...])
-    for peer in range(out_ref.shape[0]):
-        out_ref[peer] = unit
-
-
-def row_lse_kernel(demo_ref, mine_ref, other_ref, inner_ref, out_ref, top_ref, total_ref):
-    core = lax.axis_index("core")
+def prepare_kernel(both_ref, demo_out, rollout_out):
+    unit = normalize(both_ref[...])
+    share = demo_out.shape[0]
+    demo_out[...] = unit[:share]
+    for peer in range(rollout_out.shape[0]):
+        rollout_out[peer] = unit[share:]
+
+
+def row_lse_kernel(demo_ref, rollout_ref, inner_ref, out_ref, top_ref, total_ref):
     chunks, rows = inner_ref.shape[:2]
-    half = chunks // 2
-    top = None
-    for side, ref in ((core, mine_ref), (1 - core, other_ref)):
-        for c in range(half // 2):
-            inner = inner_of(demo_ref[...], ref[c * CHUNK : (c + 1) * CHUNK]) * SCALE
-            left, right = inner[:, :LANES], inner[:, LANES:]
-            inner_ref[side * half + 2 * c] = left
-            inner_ref[side * half + 2 * c + 1] = right
-            peak = jnp.maximum(left, right)
-            top_ref[...] = peak if top is None else jnp.maximum(top_ref[...], peak)
-            top = True
-
-    def add_up(b, _):
-        at = block_of(b, 64)
+    for c in range(chunks // 2):
+        inner = inner_of(demo_ref[...], rollout_ref[c * CHUNK : (c + 1) * CHUNK]) * SCALE
+        left, right = inner[:, :LANES], inner[:, LANES:]
+        inner_ref[2 * c] = left
+        inner_ref[2 * c + 1] = right
+        peak = jnp.maximum(left, right)
+        top_ref[...] = peak if c == 0 else jnp.maximum(top_ref[...], peak)
+
+    for row in range(0, rows, 64):
+        at = slice(row, row + 64)
         top = top_ref[at]
         total = jnp.zeros_like(top)
         for c in range(chunks):
             total = total + jnp.exp2(inner_ref[c, at] - top)
         total_ref[at] = total
-        return 0
-
-    lax.fori_loop(0, rows // 64, add_up, 0)
     for block in range(rows // LANES):
         at = slice(block * LANES, (block + 1) * LANES)
         top, total = top_ref[at].T, total_ref[at].T
@@ -89,32 +79,43 @@
         out_ref[:, block : block + 1] = jnp.broadcast_to(line[None], (out_ref.shape[0], 1, LANES))
 
 
-def col_lse_kernel(
-    log_rows, parts_ref, inner_ref, phi_ref, expo_ref, out_ref, column_ref, line_ref
-):
+def fold(op, values):
+    while len(values) > 1:
+        values = [op(*pair) for pair in zip(values[::2], values[1::2])]
+    return values[0]
+
+
+def col_lse_kernel(log_rows, parts_ref, inner_ref, phi_ref, column_ref, out_ref, line_ref):
     phi = -log_rows - log_total(parts_ref[...])
     phi_ref[...] = phi
     spread_rows(phi - SCALE, column_ref)
     chunks, rows = inner_ref.shape[:2]
-    width = 4
+    width, strip, strips = 4, 64, 4
 
     def group(g, _):
-        tops = [None] * width
-        for row in range(0, rows, 8):
-            at = slice(row, row + 8)
-            column = column_ref[at]
-            for w in range(width):
-                expo = inner_ref[g * width + w, at] + column
-                expo_ref[g * width + w, at] = expo
-                tops[w] = expo if row == 0 else jnp.maximum(tops[w], expo)
-        totals = [jnp.zeros((8, LANES), jnp.float32)] * width
-        for row in range(0, rows, 8):
-            for w in range(width):
-                expo = expo_ref[g * width + w, slice(row, row + 8)]
-                totals[w] = totals[w] + jnp.exp2(expo - tops[w])
+        def some_rows(b, carry):
+            tops, totals = list(carry[:width]), list(carry[width:])
+            for s in range(strips):
+                expos = [[] for _ in range(width)]
+                for row in range(0, strip, 8):
+                    at = pl.ds(pl.multiple_of((b * strips + s) * strip + row, 8), 8)
+                    column = column_ref[at]
+                    for w in range(width):
+                        expos[w].append(inner_ref[g * width + w, at] + column)
+                for w in range(width):
+                    top = jnp.maximum(tops[w], fold(jnp.maximum, expos[w]))
+                    total = fold(jnp.add, [jnp.exp2(expo - top) for expo in expos[w]])
+                    totals[w] = totals[w] * jnp.exp2(tops[w] - top) + total
+                    tops[w] = top
+            return tuple(tops + totals)
+
+        zero = jnp.zeros((8, LANES), jnp.float32)
+        carry = (zero - 1e30,) * width + (zero,) * width
+        carry = lax.fori_loop(0, rows // (strip * strips), some_rows, carry)
         for w in range(width):
-            peak = jnp.max(tops[w], axis=0, keepdims=True)
-            total = jnp.sum(totals[w] * jnp.exp2(tops[w] - peak), axis=0, keepdims=True)
+            peak = jnp.max(carry[w], axis=0, keepdims=True)
+            total = carry[width + w] * jnp.exp2(carry[w] - peak)
+            total = jnp.sum(total, axis=0, keepdims=True)
             line_ref[pl.ds(g * width + w, 1)] = peak + jnp.log2(total)
         return 0
 
@@ -122,22 +123,21 @@
     out_ref[...] = jnp.broadcast_to(line_ref[...][None], out_ref.shape)
 
 
-def row_sum_kernel(log_cols, parts_ref, expo_ref, gamma_ref, plan_ref, out_ref, total_ref):
+def row_sum_kernel(
+    log_cols, parts_ref, column_ref, inner_ref, gamma_ref, plan_ref, out_ref, total_ref
+):
     gamma = -log_cols - log_total(parts_ref[...])
     gamma_ref[...] = gamma
-    chunks, rows = expo_ref.shape[:2]
-
-    def add_up(b, _):
-        at = block_of(b, LANES)
-        total = jnp.zeros((LANES, LANES), jnp.float32)
+    chunks, rows = inner_ref.shape[:2]
+    for row in range(0, rows, LANES):
+        at = slice(row, row + LANES)
+        column = column_ref[at]
+        total = jnp.zeros_like(column)
         for c in range(chunks):
-            plan = jnp.exp2(expo_ref[c, at] + gamma[c : c + 1])
+            plan = jnp.exp2(inner_ref[c, at] + (column + gamma[c : c + 1]))
             plan_ref[c, at] = plan
             total = total + plan
         total_ref[at] = total
-        return 0
-
-    lax.fori_loop(0, rows // LANES, add_up, 0)
     for block in range(rows // LANES):
         total = total_ref[block * LANES : (block + 1) * LANES].T
         line = jnp.sum(total, axis=0, keepdims=True)
@@ -165,7 +165,7 @@
         return tuple(totals)
 
     zero = jnp.zeros((8, LANES), jnp.float32)
-    totals = lax.fori_loop(0, rows // step, add_up, (zero,) * (2 * chunks))
+    totals = lax.fori_loop(0, rows // step, add_up, (zero,) * (2 * chunks), unroll=2)
     share = LANES // 2
     low = lax.broadcasted_iota(jnp.int32, (1, LANES), 1) < share
     for c in range(chunks):
@@ -216,25 +216,28 @@
     tile = shape((cols // LANES, rows, LANES), f32)
     column = pltpu.VMEM((rows, LANES), f32)
 
-    demo_send = call(prepare_kernel, shape((n_line, share, width), bf16), [], demo)
-    rollout_send = call(prepare_kernel, shape((1, share, width), bf16), [], rollout)
-    demo_unit = lax.all_to_all(demo_send, LINE, 0, 0, tiled=True).reshape(rows, width)
-    mine = lax.all_gather(rollout_send[0], PLANE, axis=0, tiled=True)
-    other = lax.ppermute(mine, "core", [(0, 1), (1, 0)])
+    both = lax.optimization_barrier(jnp.concatenate([demo, rollout]))
+    demo_send, rollout_send = call(
+        prepare_kernel,
+        (shape((share, width), bf16), shape((n_sheet, share, width), bf16)),
+        [],
+        both,
+    )
+    rollout_unit = lax.all_to_all(rollout_send, SHEET, 0, 0, tiled=True).reshape(cols, width)
+    demo_unit = lax.all_gather(demo_send, LINE, axis=0, tiled=True)
 
     inner, row_parts = call(
         row_lse_kernel,
         (tile, shape((n_line,) + row_vec, f32)),
         [column, column],
         demo_unit,
-        mine,
-        other,
+        rollout_unit,
     )
     row_parts = lax.all_to_all(row_parts, LINE, 0, 0, tiled=True)
-    phi, expo, col_parts = call(
+    phi, spread, col_parts = call(
         functools.partial(col_lse_kernel, log_rows),
-        (shape(row_vec, f32), tile, shape((n_sheet,) + col_vec, f32)),
-        [column, pltpu.VMEM(col_vec, f32)],
+        (shape(row_vec, f32), shape((rows, LANES), f32), shape((n_sheet,) + col_vec, f32)),
+        [pltpu.VMEM(col_vec, f32)],
         row_parts,
         inner,
     )
@@ -244,7 +247,8 @@
         (shape(col_vec, f32), tile, shape((n_line,) + row_vec, f32)),
         [column],
         col_parts,
-        expo,
+        spread,
+        inner,
     )
     row_parts = lax.all_to_all(row_parts, LINE, 0, 0, tiled=True)
     phi, sums = call(

time: 123 us -> 120 us (0.976)
  blocking collectives: 84.8 us -> 97.9 us
  starting transfers between devices: 23.2 us -> 10.6 us
  waiting for transfers between devices: 1.52 us -> 0.01 us
  local copies, waits for them, and re-layouts: 1.5 us -> 0 us
    all_gather x1, blocking collectives: 20 us -> 30.3 us  [body(): demo_unit = lax.all_gather(demo_send, LINE, axis=0, tiled=True)]
    all_to_all x1, blocking collectives: 14.8 us -> 22.5 us  [body(): col_parts = lax.all_to_all(col_parts, SHEET, 0, 0, tiled=True)]
    ppermute x1 -> x0, starting transfers between devices: 7.48 us -> none  [body(): other = lax.ppermute(mine, 'core', [(0, 1), (1, 0)])]
    all_to_all x1, starting transfers between devices: 15.7 us -> 10.6 us  [body(): lax.all_to_all(rollout_send, SHEET, 0, 0, tiled=True).reshape(cols, width)]
    all_to_all x2, blocking collectives: 37.4 us -> 32.5 us  [body(): row_parts = lax.all_to_all(row_parts, LINE, 0, 0, tiled=True)]
    ppermute x1 -> x0, waiting for transfers between devices: 1.51 us -> none  [body(): other = lax.ppermute(mine, 'core', [(0, 1), (1, 0)])]
    unnamed x4 -> x0, local copies, waits for them, and re-layouts: 1.5 us -> none
    pallas_call x7 -> x6, Pallas kernels: 10.3 us -> 9.55 us  [call(): pl.pallas_call(kernel, out_shape=outs, in_specs=[VMEM] * len(args), out_s...]
  transfers between devices with their start and end apart: 2 -> 1, of which waited for: 1 -> 0; matrix products, arithmetic and copies ran while one was open for 0% -> 0% of each run, Pallas kernels for 0% -> 0%
where the time goes in v3:
time: 120 us; the launch traced here: 119 us
  blocking collectives  97.9 us (82%)
  starting transfers between devices  10.6 us (9%)
  Pallas kernels  9.55 us (8%)
    all_to_all x2, blocking collectives, body(): row_parts = lax.all_to_all(row_parts, LINE, 0, 0, tiled=True)  32.5 us
    all_gather x1, blocking collectives, body(): demo_unit = lax.all_gather(demo_send, LINE, axis=0, tiled=True)  30.3 us
    all_to_all x1, blocking collectives, body(): col_parts = lax.all_to_all(col_parts, SHEET, 0, 0, tiled=True)  22.5 us
    all_to_all x1, blocking collectives, body(): sums = lax.all_to_all(sums, SHEET, 0, 0, tiled=True)  12.6 us
    all_to_all x1, starting transfers between devices, body(): lax.all_to_all(rollout_send, SHEET, 0, 0, tiled=True).reshape(cols, width)  10.6 us
    pallas_call x6, Pallas kernels, call(): pl.pallas_call(kernel, out_shape=outs, in_specs=[VMEM] * len(args), out_s...  9.55 us
  transfers between devices with their start and end apart: 1, of which 0 were waited for; matrix products, arithmetic and copies ran while one was open for 0% of the time, Pallas kernels for 0%

profile of v3, /device:TPU:1, one launch (start us, length us, event | category | flops | bytes accessed | tf_op | source)
XLA Modules:
  0.0 119.5 jit_solution(16564387091146053368)
XLA Ops:
  0.6 0.8 pad_maximum_fusion.both_ref
  1.4 1.2 shard_map.49
  2.6 10.6 %all-to-all-start = ((bf16[32,64,256]{2,1,0:T(8,128)(2,1)}), bf16[32,64,256]{2,1,0:T(8,128)(2,1)S(1)}, u32[]{:S(2)}, u32[]{:S(2)}) async-start(bf16[32,64,256]{2,1,0:T(8,128)(2,1)} %get-tuple-element.19), calls=%async_computation | async-start | bytes 2097152 | tf_op jit(solution)/shard_map/all_to_all | solution.py:226
  13.2 30.3 %all_gather.3.demo_ref = bf16[1024,256]{1,0:T(8,128)(2,1)S(1)} all-gather(bf16[64,256]{1,0:T(8,128)(2,1)S(1)} %get-tuple-element.18), channel_id=1, replica_groups=mesh['zh'=4,'zl'=4,'core'=2,'y'=4,'x'=4] {'zh','zl'}, dimensions={0}, use_global_device_ids=true | all-gather | bytes 557056 | tf_op jit(solution)/shard_map/all_gather | solution.py:227
  43.5 0.0 all-to-all-done
  43.5 2.3 %shard_map.50 = (f32[16,1024,128]{2,1,0:T(8,128)S(1)}, f32[16,8,128]{2,1,0:T(8,128)S(1)}) custom-call(bf16[1024,256]{1,0:T(8,128)(2,1)S(1)} %all_gather.3.demo_ref, bf16[2048,256]{1,0:T(8,128)(2,1)S(1)} %bitcast.4), custom_call_target="tpu_custom_call" | custom-call | tf_op jit(solution)/shard_map/pallas_call | solution.py:198
  45.7 18.3 %all_to_all.25.parts_ref = f32[16,8,128]{2,1,0:T(8,128)S(1)} all-to-all(f32[16,8,128]{2,1,0:T(8,128)S(1)} %get-tuple-element.20), channel_id=1, replica_groups=mesh['zh'=4,'zl'=4,'core'=2,'y'=4,'x'=4] {'zh','zl'}, dimensions={0} | all-to-all | bytes 131072 | tf_op jit(solution)/shard_map/all_to_all | solution.py:236
  64.0 2.1 %shard_map.51 = (f32[8,128]{1,0:T(8,128)S(1)}, f32[1024,128]{1,0:T(8,128)S(1)}, f32[32,16,128]{2,1,0:T(8,128)S(1)}) custom-call(f32[16,8,128]{2,1,0:T(8,128)S(1)} %all_to_all.25.parts_ref, f32[16,1024,128]{2,1,0:T(8,128)S(1)} %get-tuple-element.21.inner_ref), custom_call_target="tpu_custom_call" | custom-call | tf_op jit(solution)/shard_map/pallas_call | solution.py:198
  66.1 22.5 %all_to_all.26.parts_ref = f32[32,16,128]{2,1,0:T(8,128)S(1)} all-to-all(f32[32,16,128]{2,1,0:T(8,128)S(1)} %get-tuple-element.22), channel_id=1, replica_groups=mesh['zh'=4,'zl'=4,'core'=2,'y'=4,'x'=4] {'core','y','x'}, dimensions={0} | all-to-all | bytes 524288 | tf_op jit(solution)/shard_map/all_to_all | solution.py:244
  88.6 1.4 %shard_map.52 = (f32[16,128]{1,0:T(8,128)S(1)}, f32[16,1024,128]{2,1,0:T(8,128)S(1)}, f32[16,8,128]{2,1,0:T(8,128)S(1)}) custom-call(f32[32,16,128]{2,1,0:T(8,128)S(1)} %all_to_all.26.parts_ref, f32[1024,128]{1,0:T(8,128)S(1)} %get-tuple-element.23.column_ref, f32[16,1024,128]{2,1,0:T(8,128)S(1)} %get-tuple-element.21.inner_ref), custom_call_target="tpu_custom_call" | custom-call | tf_op jit(solution)/shard_map/pallas_call | solution.py:198
  90.0 14.2 %all_to_all.27.parts_ref = f32[16,8,128]{2,1,0:T(8,128)S(1)} all-to-all(f32[16,8,128]{2,1,0:T(8,128)S(1)} %get-tuple-element.24), channel_id=1, replica_groups=mesh['zh'=4,'zl'=4,'core'=2,'y'=4,'x'=4] {'zh','zl'}, dimensions={0} | all-to-all | bytes 131072 | tf_op jit(solution)/shard_map/all_to_all | solution.py:253
  104.3 2.0 %shard_map.53 = (f32[8,128]{1,0:T(8,128)S(1)}, f32[32,1,128]{2,1,0:T(1,128)S(1)}) custom-call(f32[16,8,128]{2,1,0:T(8,128)S(1)} %all_to_all.27.parts_ref, f32[8,128]{1,0:T(8,128)S(1)} %get-tuple-element.25.phi_ref, f32[16,1024,128]{2,1,0:T(8,128)S(1)} %get-tuple-element.26.plan_ref, f32[16,1024,128]{2,1,0:T(8,128)S(1)} %get-tuple-element.21.inner_ref), custom_call_target="tpu_custom_call" | custom-call | tf_op jit(solution)/shard_map/pallas_call | solution.py:198
  106.3 12.6 %all_to_all.28.sums_ref = f32[32,1,128]{2,1,0:T(1,128)S(1)} all-to-all(f32[32,1,128]{2,1,0:T(1,128)S(1)} %get-tuple-element.27), channel_id=1, replica_groups=mesh['zh'=4,'zl'=4,'core'=2,'y'=4,'x'=4] {'core','y','x'}, dimensions={0} | all-to-all | bytes 32768 | tf_op jit(solution)/shard_map/all_to_all | solution.py:263
  118.9 0.6 shard_map.54
Async XLA Ops:
  2.6 40.9 %all-to-all-start = ((bf16[32,64,256]{2,1,0:T(8,128)(2,1)}), bf16[32,64,256]{2,1,0:T(8,128)(2,1)S(1)}, u32[]{:S(2)}, u32[]{:S(2)}) async-start(bf16[32,64,256]{2,1,0:T(8,128)(2,1)} %get-tuple-element.19), calls=%async_computation | async-start | bytes 2097152 | tf_op jit(solution)/shard_map/all_to_all | solution.py:226

commit v4 on v3

--- a/solution.py
+++ b/solution.py
@@ -17,6 +17,8 @@
 PLANE = ("y", "x")
 SHEET = ("core", "y", "x")
 LINE = ("zh", "zl")
+ROW = ("zh", "zl", "core")
+TURNS = [[2 * z + (z + turn) % 2 for z in range(16)] for turn in (0, 1)]
 ALL = ("zh", "zl", "core", "y", "x")
 VMEM = pl.BlockSpec(memory_space=pltpu.VMEM)
 PARAMS = pltpu.CompilerParams(vmem_limit_bytes=6 * 1024 * 1024)
@@ -224,7 +226,7 @@
         both,
     )
     rollout_unit = lax.all_to_all(rollout_send, SHEET, 0, 0, tiled=True).reshape(cols, width)
-    demo_unit = lax.all_gather(demo_send, LINE, axis=0, tiled=True)
+    demo_unit = lax.all_gather(demo_send, ROW, axis_index_groups=TURNS, axis=0, tiled=True)
 
     inner, row_parts = call(
         row_lse_kernel,
@@ -233,7 +235,7 @@
         demo_unit,
         rollout_unit,
     )
-    row_parts = lax.all_to_all(row_parts, LINE, 0, 0, tiled=True)
+    row_parts = lax.all_to_all(row_parts, ROW, 0, 0, axis_index_groups=TURNS, tiled=True)
     phi, spread, col_parts = call(
         functools.partial(col_lse_kernel, log_rows),
         (shape(row_vec, f32), shape((rows, LANES), f32), shape((n_sheet,) + col_vec, f32)),
@@ -250,7 +252,7 @@
         spread,
         inner,
     )
-    row_parts = lax.all_to_all(row_parts, LINE, 0, 0, tiled=True)
+    row_parts = lax.all_to_all(row_parts, ROW, 0, 0, axis_index_groups=TURNS, tiled=True)
     phi, sums = call(
         functools.partial(col_sum_kernel, log_rows),
         (shape(row_vec, f32), shape((n_sheet, 1, 2 * share), f32)),

time: 120 us -> 117 us (0.975)
  blocking collectives: 97.9 us -> 95.1 us
    all_to_all x1, blocking collectives: 22.5 us -> 16.3 us  [body(): col_parts = lax.all_to_all(col_parts, SHEET, 0, 0, tiled=True)]
    all_gather x1, blocking collectives: 30.3 us -> 33.6 us  [body(): lax.all_gather(demo_send, ROW, axis_index_groups=TURNS, axis=0, tiled=True)]
where the time goes in v4:
time: 117 us
  blocking collectives  95.1 us (81%)
  starting transfers between devices  10.6 us (9%)
  Pallas kernels  9.55 us (8%)
    all_gather x1, blocking collectives, body(): lax.all_gather(demo_send, ROW, axis_index_groups=TURNS, axis=0, tiled=True)  33.6 us
    all_to_all x2, blocking collectives, body(): lax.all_to_all(row_parts, ROW, 0, 0, axis_index_groups=TURNS, tiled=True)  33.2 us
    all_to_all x1, blocking collectives, body(): col_parts = lax.all_to_all(col_parts, SHEET, 0, 0, tiled=True)  16.3 us
    all_to_all x1, blocking collectives, body(): sums = lax.all_to_all(sums, SHEET, 0, 0, tiled=True)  11.9 us
    all_to_all x1, starting transfers between devices, body(): lax.all_to_all(rollout_send, SHEET, 0, 0, tiled=True).reshape(cols, width)  10.6 us
    pallas_call x6, Pallas kernels, call(): pl.pallas_call(kernel, out_shape=outs, in_specs=[VMEM] * len(args), out_s...  9.55 us
  transfers between devices with their start and end apart: 1, of which 0 were waited for; matrix products, arithmetic and copies ran while one was open for 0% of the time, Pallas kernels for 0%

profile of v4, /device:TPU:1, one launch (start us, length us, event | category | flops | bytes accessed | tf_op | source)
XLA Modules:
  0.0 116.7 jit_solution(9460193171849464940)
XLA Ops:
  0.6 0.8 pad_maximum_fusion.both_ref
  1.4 1.2 %shard_map.49 = (bf16[64,256]{1,0:T(8,128)(2,1)S(1)}, bf16[32,64,256]{2,1,0:T(8,128)(2,1)}) custom-call(bf16[128,256]{1,0:T(8,128)(2,1)S(1)} %pad_maximum_fusion.both_ref), custom_call_target="tpu_custom_call" | custom-call | tf_op jit(solution)/shard_map/pallas_call | solution.py:200
  2.6 10.6 %all-to-all-start = ((bf16[32,64,256]{2,1,0:T(8,128)(2,1)}), bf16[32,64,256]{2,1,0:T(8,128)(2,1)S(1)}, u32[]{:S(2)}, u32[]{:S(2)}) async-start(bf16[32,64,256]{2,1,0:T(8,128)(2,1)} %get-tuple-element.19), calls=%async_computation | async-start | bytes 2097152 | tf_op jit(solution)/shard_map/all_to_all | solution.py:228
  13.2 33.6 %all_gather.3.demo_ref = bf16[1024,256]{1,0:T(8,128)(2,1)S(1)} all-gather(bf16[64,256]{1,0:T(8,128)(2,1)S(1)} %get-tuple-element.18), channel_id=1, replica_groups={{0,48,64,112,128,176,192,240,256,304,320,368,384,432,448,496},{16,32,80..., dimensions={0}, use_global_device_ids=true | all-gather | bytes 557056 | tf_op jit(solution)/shard_map/all_gather | solution.py:229
  46.8 0.0 all-to-all-done
  46.8 2.3 %shard_map.50 = (f32[16,1024,128]{2,1,0:T(8,128)S(1)}, f32[16,8,128]{2,1,0:T(8,128)S(1)}) custom-call(bf16[1024,256]{1,0:T(8,128)(2,1)S(1)} %all_gather.3.demo_ref, bf16[2048,256]{1,0:T(8,128)(2,1)S(1)} %bitcast.4), custom_call_target="tpu_custom_call" | custom-call | tf_op jit(solution)/shard_map/pallas_call | solution.py:200
  49.1 18.0 %all_to_all.25.parts_ref = f32[16,8,128]{2,1,0:T(8,128)S(1)} all-to-all(f32[16,8,128]{2,1,0:T(8,128)S(1)} %get-tuple-element.20), channel_id=1, replica_groups={{0,48,64,112,128,176,192,240,256,304,320,368,384,432,448,496},{16,32,80..., dimensions={0} | all-to-all | bytes 131072 | tf_op jit(solution)/shard_map/all_to_all | solution.py:238
  67.1 2.1 %shard_map.51 = (f32[8,128]{1,0:T(8,128)S(1)}, f32[1024,128]{1,0:T(8,128)S(1)}, f32[32,16,128]{2,1,0:T(8,128)S(1)}) custom-call(f32[16,8,128]{2,1,0:T(8,128)S(1)} %all_to_all.25.parts_ref, f32[16,1024,128]{2,1,0:T(8,128)S(1)} %get-tuple-element.21.inner_ref), custom_call_target="tpu_custom_call" | custom-call | tf_op jit(solution)/shard_map/pallas_call | solution.py:200
  69.1 16.3 %all_to_all.26.parts_ref = f32[32,16,128]{2,1,0:T(8,128)S(1)} all-to-all(f32[32,16,128]{2,1,0:T(8,128)S(1)} %get-tuple-element.22), channel_id=1, replica_groups=mesh['zh'=4,'zl'=4,'core'=2,'y'=4,'x'=4] {'core','y','x'}, dimensions={0} | all-to-all | bytes 524288 | tf_op jit(solution)/shard_map/all_to_all | solution.py:246
  85.5 1.4 %shard_map.52 = (f32[16,128]{1,0:T(8,128)S(1)}, f32[16,1024,128]{2,1,0:T(8,128)S(1)}, f32[16,8,128]{2,1,0:T(8,128)S(1)}) custom-call(f32[32,16,128]{2,1,0:T(8,128)S(1)} %all_to_all.26.parts_ref, f32[1024,128]{1,0:T(8,128)S(1)} %get-tuple-element.23.column_ref, f32[16,1024,128]{2,1,0:T(8,128)S(1)} %get-tuple-element.21.inner_ref), custom_call_target="tpu_custom_call" | custom-call | tf_op jit(solution)/shard_map/pallas_call | solution.py:200
  86.9 15.3 %all_to_all.27.parts_ref = f32[16,8,128]{2,1,0:T(8,128)S(1)} all-to-all(f32[16,8,128]{2,1,0:T(8,128)S(1)} %get-tuple-element.24), channel_id=1, replica_groups={{0,48,64,112,128,176,192,240,256,304,320,368,384,432,448,496},{16,32,80..., dimensions={0} | all-to-all | bytes 131072 | tf_op jit(solution)/shard_map/all_to_all | solution.py:255
  102.2 2.0 %shard_map.53 = (f32[8,128]{1,0:T(8,128)S(1)}, f32[32,1,128]{2,1,0:T(1,128)S(1)}) custom-call(f32[16,8,128]{2,1,0:T(8,128)S(1)} %all_to_all.27.parts_ref, f32[8,128]{1,0:T(8,128)S(1)} %get-tuple-element.25.phi_ref, f32[16,1024,128]{2,1,0:T(8,128)S(1)} %get-tuple-element.26.plan_ref, f32[16,1024,128]{2,1,0:T(8,128)S(1)} %get-tuple-element.21.inner_ref), custom_call_target="tpu_custom_call" | custom-call | tf_op jit(solution)/shard_map/pallas_call | solution.py:200
  104.2 11.9 %all_to_all.28.sums_ref = f32[32,1,128]{2,1,0:T(1,128)S(1)} all-to-all(f32[32,1,128]{2,1,0:T(1,128)S(1)} %get-tuple-element.27), channel_id=1, replica_groups=mesh['zh'=4,'zl'=4,'core'=2,'y'=4,'x'=4] {'core','y','x'}, dimensions={0} | all-to-all | bytes 32768 | tf_op jit(solution)/shard_map/all_to_all | solution.py:265
  116.1 0.6 shard_map.54
Async XLA Ops:
  2.6 44.2 %all-to-all-start = ((bf16[32,64,256]{2,1,0:T(8,128)(2,1)}), bf16[32,64,256]{2,1,0:T(8,128)(2,1)S(1)}, u32[]{:S(2)}, u32[]{:S(2)}) async-start(bf16[32,64,256]{2,1,0:T(8,128)(2,1)} %get-tuple-element.19), calls=%async_computation | async-start | bytes 2097152 | tf_op jit(solution)/shard_map/all_to_all | solution.py:228

commit v5 on v3

--- a/solution.py
+++ b/solution.py
@@ -15,8 +15,8 @@
 LANES = 128
 CHUNK = 256
 PLANE = ("y", "x")
-SHEET = ("core", "y", "x")
-LINE = ("zh", "zl")
+SHEET = ("y", "x", "zl")
+LINE = ("zh", "core")
 ALL = ("zh", "zl", "core", "y", "x")
 VMEM = pl.BlockSpec(memory_space=pltpu.VMEM)
 PARAMS = pltpu.CompilerParams(vmem_limit_bytes=6 * 1024 * 1024)
@@ -49,8 +49,12 @@
     unit = normalize(both_ref[...])
     share = demo_out.shape[0]
     demo_out[...] = unit[:share]
-    for peer in range(rollout_out.shape[0]):
-        rollout_out[peer] = unit[share:]
+    rollout_out[...] = unit[share:]
+
+
+def copies_kernel(in_ref, out_ref):
+    for peer in range(out_ref.shape[0]):
+        out_ref[peer] = in_ref[...]
 
 
 def row_lse_kernel(demo_ref, rollout_ref, inner_ref, out_ref, top_ref, total_ref):
@@ -188,8 +192,8 @@
         total = total + sums_ref[peer]
     share = LANES // 2
     plan, cost = total[:, :share], pltpu.roll(total, share, 1)[:, :share]
-    phi_out[...] = own_half(phi_ref, lax.axis_index("zh") * 4 + lax.axis_index("zl")) * LN2
-    spot = lax.axis_index("core") * 16 + lax.axis_index("y") * 4 + lax.axis_index("x")
+    phi_out[...] = own_half(phi_ref, lax.axis_index("zh") * 2 + lax.axis_index("core")) * LN2
+    spot = lax.axis_index("y") * 8 + lax.axis_index("x") * 2 + lax.axis_index("zl")
     gamma_out[...] = (own_half(gamma_ref, spot) - log_cols - jnp.log2(plan)) * LN2
     reward_out[...] = -ratio * cost / plan
 
@@ -209,7 +213,8 @@
     f32, bf16 = jnp.float32, jnp.bfloat16
     shape = jax.ShapeDtypeStruct
     share, width = demo.shape
-    n_zh, n_line, n_sheet = lax.axis_size("zh"), lax.axis_size(LINE), lax.axis_size(SHEET)
+    n_plane = lax.axis_size(PLANE)
+    n_line, n_sheet = lax.axis_size(LINE), lax.axis_size(SHEET)
     rows, cols = share * n_line, share * n_sheet
     log_rows, log_cols = math.log2(rows * n_sheet), math.log2(cols * n_line)
     row_vec, col_vec = (rows // LANES, LANES), (cols // LANES, LANES)
@@ -217,13 +222,11 @@
     column = pltpu.VMEM((rows, LANES), f32)
 
     both = lax.optimization_barrier(jnp.concatenate([demo, rollout]))
-    demo_send, rollout_send = call(
-        prepare_kernel,
-        (shape((share, width), bf16), shape((n_sheet, share, width), bf16)),
-        [],
-        both,
-    )
-    rollout_unit = lax.all_to_all(rollout_send, SHEET, 0, 0, tiled=True).reshape(cols, width)
+    own = shape((share, width), bf16)
+    demo_send, rollout_send = call(prepare_kernel, (own, own), [], both)
+    pair = lax.all_gather(rollout_send, "zl", axis=0, tiled=True)
+    pairs = call(copies_kernel, shape((n_plane, 2 * share, width), bf16), [], pair)
+    rollout_unit = lax.all_to_all(pairs, PLANE, 0, 0, tiled=True).reshape(cols, width)
     demo_unit = lax.all_gather(demo_send, LINE, axis=0, tiled=True)
 
     inner, row_parts = call(
@@ -273,7 +276,7 @@
 
 
 def solution(mesh):
-    fine = Mesh(mesh.devices.reshape(4, 4, 2, 4, 4), ALL)
+    fine = Mesh(mesh.devices.reshape(8, 2, 2, 4, 4), ALL)
     return jax.shard_map(
         body,
         mesh=fine,

time: 120 us -> 116 us (0.967)
  starting transfers between devices: 10.6 us -> 6.75 us
    all_to_all x1, blocking collectives: 22.5 us -> 16.5 us  [body(): col_parts = lax.all_to_all(col_parts, SHEET, 0, 0, tiled=True)]
    all_gather x0 -> x1, blocking collectives: none -> 4.42 us  [body(): pair = lax.all_gather(rollout_send, 'zl', axis=0, tiled=True)]
    all_to_all x2, blocking collectives: 32.5 us -> 36.8 us  [body(): row_parts = lax.all_to_all(row_parts, LINE, 0, 0, tiled=True)]
    all_to_all x1, starting transfers between devices: 10.6 us -> 6.75 us  [body(): lax.all_to_all(pairs, PLANE, 0, 0, tiled=True).reshape(cols, width)]
    all_to_all x1, blocking collectives: 12.6 us -> 10.5 us  [body(): sums = lax.all_to_all(sums, SHEET, 0, 0, tiled=True)]
    pallas_call x6 -> x7, Pallas kernels: 9.55 us -> 9.55 us  [call(): pl.pallas_call(kernel, out_shape=outs, in_specs=[VMEM] * len(args), out_s...]
where the time goes in v5:
time: 116 us; the launch traced here: 115 us
  blocking collectives  97.5 us (84%)
  Pallas kernels  9.55 us (8%)
  starting transfers between devices  6.75 us (6%)
    all_to_all x2, blocking collectives, body(): row_parts = lax.all_to_all(row_parts, LINE, 0, 0, tiled=True)  36.8 us
    all_gather x1, blocking collectives, body(): demo_unit = lax.all_gather(demo_send, LINE, axis=0, tiled=True)  29.3 us
    all_to_all x1, blocking collectives, body(): col_parts = lax.all_to_all(col_parts, SHEET, 0, 0, tiled=True)  16.5 us
    all_to_all x1, blocking collectives, body(): sums = lax.all_to_all(sums, SHEET, 0, 0, tiled=True)  10.5 us
    pallas_call x7, Pallas kernels, call(): pl.pallas_call(kernel, out_shape=outs, in_specs=[VMEM] * len(args), out_s...  9.55 us
    all_to_all x1, starting transfers between devices, body(): lax.all_to_all(pairs, PLANE, 0, 0, tiled=True).reshape(cols, width)  6.75 us
    all_gather x1, blocking collectives, body(): pair = lax.all_gather(rollout_send, 'zl', axis=0, tiled=True)  4.42 us
  transfers between devices with their start and end apart: 1, of which 0 were waited for; matrix products, arithmetic and copies ran while one was open for 0% of the time, Pallas kernels for 0%

profile of v5, /device:TPU:1, one launch (start us, length us, event | category | flops | bytes accessed | tf_op | source)
XLA Modules:
  0.0 115.2 jit_solution(4884976489698130238)
XLA Ops:
  0.6 0.8 pad_maximum_fusion.both_ref
  1.4 0.1 shard_map.49
  1.5 4.4 %all_gather.7.in_ref = bf16[128,256]{1,0:T(8,128)(2,1)S(1)} all-gather(bf16[64,256]{1,0:T(8,128)(2,1)S(1)} %get-tuple-element.19), channel_id=1, replica_groups=mesh['zh'=8,'zl'=2,'core'=2,'y'=4,'x'=4] {'zl'}, dimensions={0}, use_global_device_ids=true | all-gather | bytes 98304 | tf_op jit(solution)/shard_map/all_gather | solution.py:227
  5.9 1.0 shard_map.50
  7.0 6.8 %all-to-all-start = ((bf16[16,128,256]{2,1,0:T(8,128)(2,1)}), bf16[16,128,256]{2,1,0:T(8,128)(2,1)S(1)}, u32[]{:S(2)}, u32[]{:S(2)}) async-start(bf16[16,128,256]{2,1,0:T(8,128)(2,1)} %shard_map.50), calls=%async_computation | async-start | bytes 2097152 | tf_op jit(solution)/shard_map/all_to_all | solution.py:229
  13.7 29.3 %all_gather.6.demo_ref = bf16[1024,256]{1,0:T(8,128)(2,1)S(1)} all-gather(bf16[64,256]{1,0:T(8,128)(2,1)S(1)} %get-tuple-element.18), channel_id=1, replica_groups=mesh['zh'=8,'zl'=2,'core'=2,'y'=4,'x'=4] {'zh','core'}, dimensions={0}, use_global_device_ids=true | all-gather | bytes 557056 | tf_op jit(solution)/shard_map/all_gather | solution.py:230
  43.0 0.0 all-to-all-done
  43.1 2.4 %shard_map.51 = (f32[16,1024,128]{2,1,0:T(8,128)S(1)}, f32[16,8,128]{2,1,0:T(8,128)S(1)}) custom-call(bf16[1024,256]{1,0:T(8,128)(2,1)S(1)} %all_gather.6.demo_ref, bf16[2048,256]{1,0:T(8,128)(2,1)S(1)} %bitcast.4), custom_call_target="tpu_custom_call" | custom-call | tf_op jit(solution)/shard_map/pallas_call | solution.py:202
  45.5 20.0 %all_to_all.25.parts_ref = f32[16,8,128]{2,1,0:T(8,128)S(1)} all-to-all(f32[16,8,128]{2,1,0:T(8,128)S(1)} %get-tuple-element.20), channel_id=1, replica_groups=mesh['zh'=8,'zl'=2,'core'=2,'y'=4,'x'=4] {'zh','core'}, dimensions={0} | all-to-all | bytes 131072 | tf_op jit(solution)/shard_map/all_to_all | solution.py:239
  65.5 2.1 %shard_map.52 = (f32[8,128]{1,0:T(8,128)S(1)}, f32[1024,128]{1,0:T(8,128)S(1)}, f32[32,16,128]{2,1,0:T(8,128)S(1)}) custom-call(f32[16,8,128]{2,1,0:T(8,128)S(1)} %all_to_all.25.parts_ref, f32[16,1024,128]{2,1,0:T(8,128)S(1)} %get-tuple-element.21.inner_ref), custom_call_target="tpu_custom_call" | custom-call | tf_op jit(solution)/shard_map/pallas_call | solution.py:202
  67.6 16.5 %all_to_all.26.parts_ref = f32[32,16,128]{2,1,0:T(8,128)S(1)} all-to-all(f32[32,16,128]{2,1,0:T(8,128)S(1)} %get-tuple-element.22), channel_id=1, replica_groups=mesh['zh'=8,'zl'=2,'core'=2,'y'=4,'x'=4] {'y','x','zl'}, dimensions={0} | all-to-all | bytes 524288 | tf_op jit(solution)/shard_map/all_to_all | solution.py:247
  84.1 1.5 %shard_map.53 = (f32[16,128]{1,0:T(8,128)S(1)}, f32[16,1024,128]{2,1,0:T(8,128)S(1)}, f32[16,8,128]{2,1,0:T(8,128)S(1)}) custom-call(f32[32,16,128]{2,1,0:T(8,128)S(1)} %all_to_all.26.parts_ref, f32[1024,128]{1,0:T(8,128)S(1)} %get-tuple-element.23.column_ref, f32[16,1024,128]{2,1,0:T(8,128)S(1)} %get-tuple-element.21.inner_ref), custom_call_target="tpu_custom_call" | custom-call | tf_op jit(solution)/shard_map/pallas_call | solution.py:202
  85.6 16.7 %all_to_all.27.parts_ref = f32[16,8,128]{2,1,0:T(8,128)S(1)} all-to-all(f32[16,8,128]{2,1,0:T(8,128)S(1)} %get-tuple-element.24), channel_id=1, replica_groups=mesh['zh'=8,'zl'=2,'core'=2,'y'=4,'x'=4] {'zh','core'}, dimensions={0} | all-to-all | bytes 131072 | tf_op jit(solution)/shard_map/all_to_all | solution.py:256
  102.3 1.9 %shard_map.54 = (f32[8,128]{1,0:T(8,128)S(1)}, f32[32,1,128]{2,1,0:T(1,128)S(1)}) custom-call(f32[16,8,128]{2,1,0:T(8,128)S(1)} %all_to_all.27.parts_ref, f32[8,128]{1,0:T(8,128)S(1)} %get-tuple-element.25.phi_ref, f32[16,1024,128]{2,1,0:T(8,128)S(1)} %get-tuple-element.26.plan_ref, f32[16,1024,128]{2,1,0:T(8,128)S(1)} %get-tuple-element.21.inner_ref), custom_call_target="tpu_custom_call" | custom-call | tf_op jit(solution)/shard_map/pallas_call | solution.py:202
  104.2 10.5 %all_to_all.28.sums_ref = f32[32,1,128]{2,1,0:T(1,128)S(1)} all-to-all(f32[32,1,128]{2,1,0:T(1,128)S(1)} %get-tuple-element.27), channel_id=1, replica_groups=mesh['zh'=8,'zl'=2,'core'=2,'y'=4,'x'=4] {'y','x','zl'}, dimensions={0} | all-to-all | bytes 32768 | tf_op jit(solution)/shard_map/all_to_all | solution.py:266
  114.6 0.6 shard_map.55
Async XLA Ops:
  7.0 36.1 %all-to-all-start = ((bf16[16,128,256]{2,1,0:T(8,128)(2,1)}), bf16[16,128,256]{2,1,0:T(8,128)(2,1)S(1)}, u32[]{:S(2)}, u32[]{:S(2)}) async-start(bf16[16,128,256]{2,1,0:T(8,128)(2,1)} %shard_map.50), calls=%async_computation | async-start | bytes 2097152 | tf_op jit(solution)/shard_map/all_to_all | solution.py:229

commit v6 on v5

--- a/solution.py
+++ b/solution.py
@@ -142,16 +142,23 @@
             plan_ref[c, at] = plan
             total = total + plan
         total_ref[at] = total
+    lines = []
     for block in range(rows // LANES):
         total = total_ref[block * LANES : (block + 1) * LANES].T
-        line = jnp.sum(total, axis=0, keepdims=True)
-        out_ref[:, block : block + 1] = jnp.broadcast_to(line[None], (out_ref.shape[0], 1, LANES))
+        lines.append(jnp.sum(total, axis=0, keepdims=True))
+    peers = out_ref.shape[0] // len(lines)
+    out_ref[...] = jnp.concatenate(lines * peers).astype(out_ref.dtype)
 
 
 def col_sum_kernel(
     log_rows, parts_ref, phi_ref, plan_ref, inner_ref, phi_out, out_ref, column_ref
 ):
-    change = -log_rows - jnp.log2(jnp.sum(parts_ref[...], axis=0))
+    blocks = phi_ref.shape[0]
+    parts = parts_ref[...].astype(jnp.float32)
+    total = parts[:blocks]
+    for peer in range(1, parts.shape[0] // blocks):
+        total = total + parts[peer * blocks : (peer + 1) * blocks]
+    change = -log_rows - jnp.log2(total)
     phi_out[...] = phi_ref[...] + change
     spread_rows(jnp.exp2(change), column_ref)
     chunks, rows = plan_ref.shape[:2]
@@ -247,13 +254,15 @@
     col_parts = lax.all_to_all(col_parts, SHEET, 0, 0, tiled=True)
     gamma, plan, row_parts = call(
         functools.partial(row_sum_kernel, log_cols),
-        (shape(col_vec, f32), tile, shape((n_line,) + row_vec, f32)),
+        (shape(col_vec, f32), tile, shape((n_line * row_vec[0], LANES), bf16)),
         [column],
         col_parts,
         spread,
         inner,
     )
+    row_parts = row_parts.reshape((n_line,) + row_vec)
     row_parts = lax.all_to_all(row_parts, LINE, 0, 0, tiled=True)
+    row_parts = row_parts.reshape(n_line * row_vec[0], LANES)
     phi, sums = call(
         functools.partial(col_sum_kernel, log_rows),
         (shape(row_vec, f32), shape((n_sheet, 1, 2 * share), f32)),

time: 116 us -> 114 us (0.983)
  blocking collectives: 97.5 us -> 96.2 us
where the time goes in v6:
time: 114 us
  blocking collectives  96.2 us (84%)
  Pallas kernels  9.53 us (8%)
  starting transfers between devices  6.75 us (6%)
    all_to_all x2, blocking collectives, body(): row_parts = lax.all_to_all(row_parts, LINE, 0, 0, tiled=True)  35.7 us
    all_gather x1, blocking collectives, body(): demo_unit = lax.all_gather(demo_send, LINE, axis=0, tiled=True)  29.3 us
    all_to_all x1, blocking collectives, body(): col_parts = lax.all_to_all(col_parts, SHEET, 0, 0, tiled=True)  16.5 us
    all_to_all x1, blocking collectives, body(): sums = lax.all_to_all(sums, SHEET, 0, 0, tiled=True)  10.3 us
    pallas_call x7, Pallas kernels, call(): pl.pallas_call(kernel, out_shape=outs, in_specs=[VMEM] * len(args), out_s...  9.53 us
    all_to_all x1, starting transfers between devices, body(): lax.all_to_all(pairs, PLANE, 0, 0, tiled=True).reshape(cols, width)  6.75 us
    all_gather x1, blocking collectives, body(): pair = lax.all_gather(rollout_send, 'zl', axis=0, tiled=True)  4.42 us
  transfers between devices with their start and end apart: 1, of which 0 were waited for; matrix products, arithmetic and copies ran while one was open for 0% of the time, Pallas kernels for 0%

profile of v6, /device:TPU:1, one launch (start us, length us, event | category | flops | bytes accessed | tf_op | source)
XLA Modules:
  0.0 114.0 jit_solution(16650944701571929295)
XLA Ops:
  0.6 0.8 pad_maximum_fusion.both_ref
  1.4 0.1 shard_map.49
  1.5 4.4 %all_gather.7.in_ref = bf16[128,256]{1,0:T(8,128)(2,1)S(1)} all-gather(bf16[64,256]{1,0:T(8,128)(2,1)S(1)} %get-tuple-element.19), channel_id=1, replica_groups=mesh['zh'=8,'zl'=2,'core'=2,'y'=4,'x'=4] {'zl'}, dimensions={0}, use_global_device_ids=true | all-gather | bytes 98304 | tf_op jit(solution)/shard_map/all_gather | solution.py:234
  5.9 1.0 shard_map.50
  7.0 6.8 %all-to-all-start = ((bf16[16,128,256]{2,1,0:T(8,128)(2,1)}), bf16[16,128,256]{2,1,0:T(8,128)(2,1)S(1)}, u32[]{:S(2)}, u32[]{:S(2)}) async-start(bf16[16,128,256]{2,1,0:T(8,128)(2,1)} %shard_map.50), calls=%async_computation | async-start | bytes 2097152 | tf_op jit(solution)/shard_map/all_to_all | solution.py:236
  13.7 29.3 %all_gather.6.demo_ref = bf16[1024,256]{1,0:T(8,128)(2,1)S(1)} all-gather(bf16[64,256]{1,0:T(8,128)(2,1)S(1)} %get-tuple-element.18), channel_id=1, replica_groups=mesh['zh'=8,'zl'=2,'core'=2,'y'=4,'x'=4] {'zh','core'}, dimensions={0}, use_global_device_ids=true | all-gather | bytes 557056 | tf_op jit(solution)/shard_map/all_gather | solution.py:237
  43.0 0.0 all-to-all-done
  43.1 2.3 %shard_map.51 = (f32[16,1024,128]{2,1,0:T(8,128)S(1)}, f32[16,8,128]{2,1,0:T(8,128)S(1)}) custom-call(bf16[1024,256]{1,0:T(8,128)(2,1)S(1)} %all_gather.6.demo_ref, bf16[2048,256]{1,0:T(8,128)(2,1)S(1)} %bitcast.6), custom_call_target="tpu_custom_call" | custom-call | tf_op jit(solution)/shard_map/pallas_call | solution.py:209
  45.3 20.0 %all_to_all.25.parts_ref = f32[16,8,128]{2,1,0:T(8,128)S(1)} all-to-all(f32[16,8,128]{2,1,0:T(8,128)S(1)} %get-tuple-element.20), channel_id=1, replica_groups=mesh['zh'=8,'zl'=2,'core'=2,'y'=4,'x'=4] {'zh','core'}, dimensions={0} | all-to-all | bytes 131072 | tf_op jit(solution)/shard_map/all_to_all | solution.py:246
  65.4 2.1 %shard_map.52 = (f32[8,128]{1,0:T(8,128)S(1)}, f32[1024,128]{1,0:T(8,128)S(1)}, f32[32,16,128]{2,1,0:T(8,128)S(1)}) custom-call(f32[16,8,128]{2,1,0:T(8,128)S(1)} %all_to_all.25.parts_ref, f32[16,1024,128]{2,1,0:T(8,128)S(1)} %get-tuple-element.21.inner_ref), custom_call_target="tpu_custom_call" | custom-call | tf_op jit(solution)/shard_map/pallas_call | solution.py:209
  67.5 16.5 %all_to_all.26.parts_ref = f32[32,16,128]{2,1,0:T(8,128)S(1)} all-to-all(f32[32,16,128]{2,1,0:T(8,128)S(1)} %get-tuple-element.22), channel_id=1, replica_groups=mesh['zh'=8,'zl'=2,'core'=2,'y'=4,'x'=4] {'y','x','zl'}, dimensions={0} | all-to-all | bytes 524288 | tf_op jit(solution)/shard_map/all_to_all | solution.py:254
  84.0 1.4 %shard_map.53 = (f32[16,128]{1,0:T(8,128)S(1)}, f32[16,1024,128]{2,1,0:T(8,128)S(1)}, bf16[128,128]{1,0:T(8,128)(2,1)S(1)}) custom-call(f32[32,16,128]{2,1,0:T(8,128)S(1)} %all_to_all.26.parts_ref, f32[1024,128]{1,0:T(8,128)S(1)} %get-tuple-element.23.column_ref, f32[16,1024,128]{2,1,0:T(8,128)S(1)} %get-tuple-element.21.inner_ref), custom_call_target="tpu_custom_call" | custom-call | tf_op jit(solution)/shard_map/pallas_call | solution.py:209
  85.4 15.7 %all_to_all.27 = bf16[16,8,128]{2,1,0:T(8,128)(2,1)S(1)} all-to-all(bf16[16,8,128]{2,1,0:T(8,128)(2,1)S(1)} %bitcast.8), channel_id=1, replica_groups=mesh['zh'=8,'zl'=2,'core'=2,'y'=4,'x'=4] {'zh','core'}, dimensions={0} | all-to-all | bytes 65536 | tf_op jit(solution)/shard_map/all_to_all | solution.py:264
  101.1 2.0 %shard_map.54 = (f32[8,128]{1,0:T(8,128)S(1)}, f32[32,1,128]{2,1,0:T(1,128)S(1)}) custom-call(bf16[128,128]{1,0:T(8,128)(2,1)S(1)} %bitcast.7, f32[8,128]{1,0:T(8,128)S(1)} %get-tuple-element.25.phi_ref, f32[16,1024,128]{2,1,0:T(8,128)S(1)} %get-tuple-element.26.plan_ref, f32[16,1024,128]{2,1,0:T(8,128)S(1)} %get-tuple-element.21.inner_ref), custom_call_target="tpu_custom_call" | custom-call | tf_op jit(solution)/shard_map/pallas_call | solution.py:209
  103.1 10.3 %all_to_all.28.sums_ref = f32[32,1,128]{2,1,0:T(1,128)S(1)} all-to-all(f32[32,1,128]{2,1,0:T(1,128)S(1)} %get-tuple-element.27), channel_id=1, replica_groups=mesh['zh'=8,'zl'=2,'core'=2,'y'=4,'x'=4] {'y','x','zl'}, dimensions={0} | all-to-all | bytes 32768 | tf_op jit(solution)/shard_map/all_to_all | solution.py:275
  113.4 0.6 shard_map.55
Async XLA Ops:
  7.0 36.1 %all-to-all-start = ((bf16[16,128,256]{2,1,0:T(8,128)(2,1)}), bf16[16,128,256]{2,1,0:T(8,128)(2,1)S(1)}, u32[]{:S(2)}, u32[]{:S(2)}) async-start(bf16[16,128,256]{2,1,0:T(8,128)(2,1)} %shard_map.50), calls=%async_computation | async-start | bytes 2097152 | tf_op jit(solution)/shard_map/all_to_all | solution.py:236

commit v7 on v6

--- a/solution.py
+++ b/solution.py
@@ -45,20 +45,18 @@
         column_ref[block * LANES : (block + 1) * LANES] = wide.T
 
 
-def prepare_kernel(both_ref, demo_out, rollout_out):
-    unit = normalize(both_ref[...])
-    share = demo_out.shape[0]
-    demo_out[...] = unit[:share]
-    rollout_out[...] = unit[share:]
-
-
-def copies_kernel(in_ref, out_ref):
-    for peer in range(out_ref.shape[0]):
-        out_ref[peer] = in_ref[...]
-
-
-def row_lse_kernel(demo_ref, rollout_ref, inner_ref, out_ref, top_ref, total_ref):
+def prepare_kernel(pair_ref, pair_out):
+    pair = normalize(pair_ref[...])
+    for peer in range(pair_out.shape[0]):
+        pair_out[peer] = pair
+
+
+def row_lse_kernel(
+    raw_ref, rollout_ref, inner_ref, out_ref, demo_ref, top_ref, total_ref
+):
     chunks, rows = inner_ref.shape[:2]
+    for row in range(0, rows, LANES):
+        demo_ref[row : row + LANES] = normalize(raw_ref[row : row + LANES])
     for c in range(chunks // 2):
         inner = inner_of(demo_ref[...], rollout_ref[c * CHUNK : (c + 1) * CHUNK]) * SCALE
         left, right = inner[:, :LANES], inner[:, LANES:]
@@ -228,18 +226,15 @@
     tile = shape((cols // LANES, rows, LANES), f32)
     column = pltpu.VMEM((rows, LANES), f32)
 
-    both = lax.optimization_barrier(jnp.concatenate([demo, rollout]))
-    own = shape((share, width), bf16)
-    demo_send, rollout_send = call(prepare_kernel, (own, own), [], both)
-    pair = lax.all_gather(rollout_send, "zl", axis=0, tiled=True)
-    pairs = call(copies_kernel, shape((n_plane, 2 * share, width), bf16), [], pair)
+    pair = lax.all_gather(rollout, "zl", axis=0, tiled=True)
+    pairs = call(prepare_kernel, shape((n_plane, 2 * share, width), bf16), [], pair)
     rollout_unit = lax.all_to_all(pairs, PLANE, 0, 0, tiled=True).reshape(cols, width)
-    demo_unit = lax.all_gather(demo_send, LINE, axis=0, tiled=True)
+    demo_unit = lax.all_gather(demo, LINE, axis=0, tiled=True)
 
     inner, row_parts = call(
         row_lse_kernel,
         (tile, shape((n_line,) + row_vec, f32)),
-        [column, column],
+        [pltpu.VMEM((rows, width), bf16), column, column],
         demo_unit,
         rollout_unit,
     )

time: 114 us -> 114 us (level)
    pallas_call x7 -> x6, Pallas kernels: 9.53 us -> 9.58 us  [call(): pl.pallas_call(kernel, out_shape=outs, in_specs=[VMEM] * len(args), out_s...]
where the time goes in v7:
time: 114 us
  blocking collectives  96.7 us (85%)
  Pallas kernels  9.58 us (8%)
  starting transfers between devices  6.75 us (6%)
    all_to_all x2, blocking collectives, body(): row_parts = lax.all_to_all(row_parts, LINE, 0, 0, tiled=True)  35.8 us
    all_gather x1, blocking collectives, body(): demo_unit = lax.all_gather(demo, LINE, axis=0, tiled=True)  29.5 us
    all_to_all x1, blocking collectives, body(): col_parts = lax.all_to_all(col_parts, SHEET, 0, 0, tiled=True)  16.5 us
    all_to_all x1, blocking collectives, body(): sums = lax.all_to_all(sums, SHEET, 0, 0, tiled=True)  10.3 us
    pallas_call x6, Pallas kernels, call(): pl.pallas_call(kernel, out_shape=outs, in_specs=[VMEM] * len(args), out_s...  9.58 us
    all_to_all x1, starting transfers between devices, body(): lax.all_to_all(pairs, PLANE, 0, 0, tiled=True).reshape(cols, width)  6.75 us
    all_gather x1, blocking collectives, body(): pair = lax.all_gather(rollout, 'zl', axis=0, tiled=True)  4.7 us
  transfers between devices with their start and end apart: 1, of which 0 were waited for; matrix products, arithmetic and copies ran while one was open for 0% of the time, Pallas kernels for 0%

profile of v7, /device:TPU:1, one launch (start us, length us, event | category | flops | bytes accessed | tf_op | source)
XLA Modules:
  0.0 113.7 jit_solution(10464220918824266955)
XLA Ops:
  0.6 4.7 %all_gather.7.pair_ref = bf16[128,256]{1,0:T(8,128)(2,1)S(1)} all-gather(bf16[64,256]{1,0:T(8,128)(2,1)} %param.3), channel_id=1, replica_groups=mesh['zh'=8,'zl'=2,'core'=2,'y'=4,'x'=4] {'zl'}, dimensions={0}, use_global_device_ids=true | all-gather | bytes 98304 | tf_op jit(solution)/shard_map/all_gather | solution.py:229
  5.3 1.2 %shard_map.49 = bf16[16,128,256]{2,1,0:T(8,128)(2,1)} custom-call(bf16[128,256]{1,0:T(8,128)(2,1)S(1)} %all_gather.7.pair_ref), custom_call_target="tpu_custom_call" | custom-call | tf_op jit(solution)/shard_map/pallas_call | solution.py:207
  6.5 6.8 %all-to-all-start = ((bf16[16,128,256]{2,1,0:T(8,128)(2,1)}), bf16[16,128,256]{2,1,0:T(8,128)(2,1)S(1)}, u32[]{:S(2)}, u32[]{:S(2)}) async-start(bf16[16,128,256]{2,1,0:T(8,128)(2,1)} %shard_map.49), calls=%async_computation | async-start | bytes 2097152 | tf_op jit(solution)/shard_map/all_to_all | solution.py:231
  13.3 29.5 %all_gather.6.raw_ref = bf16[1024,256]{1,0:T(8,128)(2,1)S(1)} all-gather(bf16[64,256]{1,0:T(8,128)(2,1)} %param.2), channel_id=1, replica_groups=mesh['zh'=8,'zl'=2,'core'=2,'y'=4,'x'=4] {'zh','core'}, dimensions={0}, use_global_device_ids=true | all-gather | bytes 557056 | tf_op jit(solution)/shard_map/all_gather | solution.py:232
  42.7 0.0 all-to-all-done
  42.7 2.4 %shard_map.50 = (f32[16,1024,128]{2,1,0:T(8,128)S(1)}, f32[16,8,128]{2,1,0:T(8,128)S(1)}) custom-call(bf16[1024,256]{1,0:T(8,128)(2,1)S(1)} %all_gather.6.raw_ref, bf16[2048,256]{1,0:T(8,128)(2,1)S(1)} %bitcast.6), custom_call_target="tpu_custom_call" | custom-call | tf_op jit(solution)/shard_map/pallas_call | solution.py:207
  45.2 20.1 %all_to_all.25.parts_ref = f32[16,8,128]{2,1,0:T(8,128)S(1)} all-to-all(f32[16,8,128]{2,1,0:T(8,128)S(1)} %get-tuple-element.16), channel_id=1, replica_groups=mesh['zh'=8,'zl'=2,'core'=2,'y'=4,'x'=4] {'zh','core'}, dimensions={0} | all-to-all | bytes 131072 | tf_op jit(solution)/shard_map/all_to_all | solution.py:241
  65.2 2.1 %shard_map.51 = (f32[8,128]{1,0:T(8,128)S(1)}, f32[1024,128]{1,0:T(8,128)S(1)}, f32[32,16,128]{2,1,0:T(8,128)S(1)}) custom-call(f32[16,8,128]{2,1,0:T(8,128)S(1)} %all_to_all.25.parts_ref, f32[16,1024,128]{2,1,0:T(8,128)S(1)} %get-tuple-element.17.inner_ref), custom_call_target="tpu_custom_call" | custom-call | tf_op jit(solution)/shard_map/pallas_call | solution.py:207
  67.3 16.5 %all_to_all.26.parts_ref = f32[32,16,128]{2,1,0:T(8,128)S(1)} all-to-all(f32[32,16,128]{2,1,0:T(8,128)S(1)} %get-tuple-element.18), channel_id=1, replica_groups=mesh['zh'=8,'zl'=2,'core'=2,'y'=4,'x'=4] {'y','x','zl'}, dimensions={0} | all-to-all | bytes 524288 | tf_op jit(solution)/shard_map/all_to_all | solution.py:249
  83.8 1.5 %shard_map.52 = (f32[16,128]{1,0:T(8,128)S(1)}, f32[16,1024,128]{2,1,0:T(8,128)S(1)}, bf16[128,128]{1,0:T(8,128)(2,1)S(1)}) custom-call(f32[32,16,128]{2,1,0:T(8,128)S(1)} %all_to_all.26.parts_ref, f32[1024,128]{1,0:T(8,128)S(1)} %get-tuple-element.19.column_ref, f32[16,1024,128]{2,1,0:T(8,128)S(1)} %get-tuple-element.17.inner_ref), custom_call_target="tpu_custom_call" | custom-call | tf_op jit(solution)/shard_map/pallas_call | solution.py:207
  85.2 15.7 %all_to_all.27 = bf16[16,8,128]{2,1,0:T(8,128)(2,1)S(1)} all-to-all(bf16[16,8,128]{2,1,0:T(8,128)(2,1)S(1)} %bitcast.8), channel_id=1, replica_groups=mesh['zh'=8,'zl'=2,'core'=2,'y'=4,'x'=4] {'zh','core'}, dimensions={0} | all-to-all | bytes 65536 | tf_op jit(solution)/shard_map/all_to_all | solution.py:259
  100.9 1.9 %shard_map.53 = (f32[8,128]{1,0:T(8,128)S(1)}, f32[32,1,128]{2,1,0:T(1,128)S(1)}) custom-call(bf16[128,128]{1,0:T(8,128)(2,1)S(1)} %bitcast.7, f32[8,128]{1,0:T(8,128)S(1)} %get-tuple-element.21.phi_ref, f32[16,1024,128]{2,1,0:T(8,128)S(1)} %get-tuple-element.22.plan_ref, f32[16,1024,128]{2,1,0:T(8,128)S(1)} %get-tuple-element.17.inner_ref), custom_call_target="tpu_custom_call" | custom-call | tf_op jit(solution)/shard_map/pallas_call | solution.py:207
  102.8 10.3 %all_to_all.28.sums_ref = f32[32,1,128]{2,1,0:T(1,128)S(1)} all-to-all(f32[32,1,128]{2,1,0:T(1,128)S(1)} %get-tuple-element.23), channel_id=1, replica_groups=mesh['zh'=8,'zl'=2,'core'=2,'y'=4,'x'=4] {'y','x','zl'}, dimensions={0} | all-to-all | bytes 32768 | tf_op jit(solution)/shard_map/all_to_all | solution.py:270
  113.1 0.6 shard_map.54
Async XLA Ops:
  6.5 36.3 %all-to-all-start = ((bf16[16,128,256]{2,1,0:T(8,128)(2,1)}), bf16[16,128,256]{2,1,0:T(8,128)(2,1)S(1)}, u32[]{:S(2)}, u32[]{:S(2)}) async-start(bf16[16,128,256]{2,1,0:T(8,128)(2,1)} %shard_map.49), calls=%async_computation | async-start | bytes 2097152 | tf_op jit(solution)/shard_map/all_to_all | solution.py:231

commit v8 on v7

--- a/solution.py
+++ b/solution.py
@@ -39,6 +39,10 @@
     return top + jnp.log2(jnp.sum(jnp.exp2(parts - top[None]), axis=0))
 
 
+def lanes(chunk):
+    return slice(chunk * LANES, (chunk + 1) * LANES)
+
+
 def spread_rows(vector, column_ref):
     for block in range(vector.shape[0]):
         wide = jnp.broadcast_to(vector[block : block + 1], (LANES, LANES))
@@ -54,15 +58,13 @@
 def row_lse_kernel(
     raw_ref, rollout_ref, inner_ref, out_ref, demo_ref, top_ref, total_ref
 ):
-    chunks, rows = inner_ref.shape[:2]
+    rows, chunks = inner_ref.shape[0], inner_ref.shape[1] // LANES
     for row in range(0, rows, LANES):
         demo_ref[row : row + LANES] = normalize(raw_ref[row : row + LANES])
     for c in range(chunks // 2):
         inner = inner_of(demo_ref[...], rollout_ref[c * CHUNK : (c + 1) * CHUNK]) * SCALE
-        left, right = inner[:, :LANES], inner[:, LANES:]
-        inner_ref[2 * c] = left
-        inner_ref[2 * c + 1] = right
-        peak = jnp.maximum(left, right)
+        inner_ref[:, c * CHUNK : (c + 1) * CHUNK] = inner
+        peak = jnp.maximum(inner[:, :LANES], inner[:, LANES:])
         top_ref[...] = peak if c == 0 else jnp.maximum(top_ref[...], peak)
 
     for row in range(0, rows, 64):
@@ -70,7 +72,7 @@
         top = top_ref[at]
         total = jnp.zeros_like(top)
         for c in range(chunks):
-            total = total + jnp.exp2(inner_ref[c, at] - top)
+            total = total + jnp.exp2(inner_ref[at, lanes(c)] - top)
         total_ref[at] = total
     for block in range(rows // LANES):
         at = slice(block * LANES, (block + 1) * LANES)
@@ -91,11 +93,12 @@
     phi = -log_rows - log_total(parts_ref[...])
     phi_ref[...] = phi
     spread_rows(phi - SCALE, column_ref)
-    chunks, rows = inner_ref.shape[:2]
+    rows, chunks = inner_ref.shape[0], inner_ref.shape[1] // LANES
     width, strip, strips = 4, 64, 4
 
-    def group(g, _):
-        def some_rows(b, carry):
+    for g in range(chunks // width):
+
+        def some_rows(b, carry, g=g):
             tops, totals = list(carry[:width]), list(carry[width:])
             for s in range(strips):
                 expos = [[] for _ in range(width)]
@@ -103,7 +106,7 @@
                     at = pl.ds(pl.multiple_of((b * strips + s) * strip + row, 8), 8)
                     column = column_ref[at]
                     for w in range(width):
-                        expos[w].append(inner_ref[g * width + w, at] + column)
+                        expos[w].append(inner_ref[at, lanes(g * width + w)] + column)
                 for w in range(width):
                     top = jnp.maximum(tops[w], fold(jnp.maximum, expos[w]))
                     total = fold(jnp.add, [jnp.exp2(expo - top) for expo in expos[w]])
@@ -113,15 +116,12 @@
 
         zero = jnp.zeros((8, LANES), jnp.float32)
         carry = (zero - 1e30,) * width + (zero,) * width
-        carry = lax.fori_loop(0, rows // (strip * strips), some_rows, carry)
+        carry = lax.fori_loop(0, rows // (strip * strips), some_rows, carry, unroll=4)
         for w in range(width):
             peak = jnp.max(carry[w], axis=0, keepdims=True)
             total = carry[width + w] * jnp.exp2(carry[w] - peak)
             total = jnp.sum(total, axis=0, keepdims=True)
-            line_ref[pl.ds(g * width + w, 1)] = peak + jnp.log2(total)
-        return 0
-
-    lax.fori_loop(0, chunks // width, group, 0)
+            line_ref[g * width + w : g * width + w + 1] = peak + jnp.log2(total)
     out_ref[...] = jnp.broadcast_to(line_ref[...][None], out_ref.shape)
 
 
@@ -130,14 +130,14 @@
 ):
     gamma = -log_cols - log_total(parts_ref[...])
     gamma_ref[...] = gamma
-    chunks, rows = inner_ref.shape[:2]
+    rows, chunks = inner_ref.shape[0], inner_ref.shape[1] // LANES
     for row in range(0, rows, LANES):
         at = slice(row, row + LANES)
         column = column_ref[at]
         total = jnp.zeros_like(column)
         for c in range(chunks):
-            plan = jnp.exp2(inner_ref[c, at] + (column + gamma[c : c + 1]))
-            plan_ref[c, at] = plan
+            plan = jnp.exp2(inner_ref[at, lanes(c)] + (column + gamma[c : c + 1]))
+            plan_ref[at, lanes(c)] = plan
             total = total + plan
         total_ref[at] = total
     lines = []
@@ -159,18 +159,20 @@
     change = -log_rows - jnp.log2(total)
     phi_out[...] = phi_ref[...] + change
     spread_rows(jnp.exp2(change), column_ref)
-    chunks, rows = plan_ref.shape[:2]
+    rows, chunks = plan_ref.shape[0], plan_ref.shape[1] // LANES
     step = 128
 
     def add_up(b, totals):
         totals = list(totals)
-        for row in range(0, step, 8):
-            at = pl.ds(pl.multiple_of(b * step + row, 8), 8)
-            column = column_ref[at]
+        for row in range(0, step, 16):
+            one = pl.ds(pl.multiple_of(b * step + row, 8), 8)
+            two = pl.ds(pl.multiple_of(b * step + row + 8, 8), 8)
             for c in range(chunks):
-                plan = plan_ref[c, at] * column
-                totals[c] = totals[c] + plan
-                totals[chunks + c] = totals[chunks + c] + plan * (SCALE - inner_ref[c, at])
+                at = lanes(c)
+                plan, plan2 = plan_ref[one, at] * column_ref[one], plan_ref[two, at] * column_ref[two]
+                cost = plan * (SCALE - inner_ref[one, at]) + plan2 * (SCALE - inner_ref[two, at])
+                totals[c] = totals[c] + (plan + plan2)
+                totals[chunks + c] = totals[chunks + c] + cost
         return tuple(totals)
 
     zero = jnp.zeros((8, LANES), jnp.float32)
@@ -223,7 +225,7 @@
     rows, cols = share * n_line, share * n_sheet
     log_rows, log_cols = math.log2(rows * n_sheet), math.log2(cols * n_line)
     row_vec, col_vec = (rows // LANES, LANES), (cols // LANES, LANES)
-    tile = shape((cols // LANES, rows, LANES), f32)
+    tile = shape((rows, cols), f32)
     column = pltpu.VMEM((rows, LANES), f32)
 
     pair = lax.all_gather(rollout, "zl", axis=0, tiled=True)

time: 114 us -> 114 us (level)
  no operation moved by 1% of the time
where the time goes in v8:
time: 114 us; the launch traced here: 113 us
  blocking collectives  96.7 us (85%)
  Pallas kernels  9.36 us (8%)
  starting transfers between devices  6.75 us (6%)
    all_to_all x2, blocking collectives, body(): row_parts = lax.all_to_all(row_parts, LINE, 0, 0, tiled=True)  35.8 us
    all_gather x1, blocking collectives, body(): demo_unit = lax.all_gather(demo, LINE, axis=0, tiled=True)  29.5 us
    all_to_all x1, blocking collectives, body(): col_parts = lax.all_to_all(col_parts, SHEET, 0, 0, tiled=True)  16.5 us
    all_to_all x1, blocking collectives, body(): sums = lax.all_to_all(sums, SHEET, 0, 0, tiled=True)  10.3 us
    pallas_call x6, Pallas kernels, call(): pl.pallas_call(kernel, out_shape=outs, in_specs=[VMEM] * len(args), out_s...  9.36 us
    all_to_all x1, starting transfers between devices, body(): lax.all_to_all(pairs, PLANE, 0, 0, tiled=True).reshape(cols, width)  6.75 us
    all_gather x1, blocking collectives, body(): pair = lax.all_gather(rollout, 'zl', axis=0, tiled=True)  4.7 us
  transfers between devices with their start and end apart: 1, of which 0 were waited for; matrix products, arithmetic and copies ran while one was open for 0% of the time, Pallas kernels for 0%

profile of v8, /device:TPU:1, one launch (start us, length us, event | category | flops | bytes accessed | tf_op | source)
XLA Modules:
  0.0 113.5 jit_solution(6425337127952549619)
XLA Ops:
  0.6 4.7 %all_gather.7.pair_ref = bf16[128,256]{1,0:T(8,128)(2,1)S(1)} all-gather(bf16[64,256]{1,0:T(8,128)(2,1)} %param.3), channel_id=1, replica_groups=mesh['zh'=8,'zl'=2,'core'=2,'y'=4,'x'=4] {'zl'}, dimensions={0}, use_global_device_ids=true | all-gather | bytes 98304 | tf_op jit(solution)/shard_map/all_gather | solution.py:231
  5.3 1.2 %shard_map.49 = bf16[16,128,256]{2,1,0:T(8,128)(2,1)} custom-call(bf16[128,256]{1,0:T(8,128)(2,1)S(1)} %all_gather.7.pair_ref), custom_call_target="tpu_custom_call" | custom-call | tf_op jit(solution)/shard_map/pallas_call | solution.py:209
  6.5 6.8 %all-to-all-start = ((bf16[16,128,256]{2,1,0:T(8,128)(2,1)}), bf16[16,128,256]{2,1,0:T(8,128)(2,1)S(1)}, u32[]{:S(2)}, u32[]{:S(2)}) async-start(bf16[16,128,256]{2,1,0:T(8,128)(2,1)} %shard_map.49), calls=%async_computation | async-start | bytes 2097152 | tf_op jit(solution)/shard_map/all_to_all | solution.py:233
  13.3 29.5 %all_gather.6.raw_ref = bf16[1024,256]{1,0:T(8,128)(2,1)S(1)} all-gather(bf16[64,256]{1,0:T(8,128)(2,1)} %param.2), channel_id=1, replica_groups=mesh['zh'=8,'zl'=2,'core'=2,'y'=4,'x'=4] {'zh','core'}, dimensions={0}, use_global_device_ids=true | all-gather | bytes 557056 | tf_op jit(solution)/shard_map/all_gather | solution.py:234
  42.7 0.0 all-to-all-done
  42.7 2.4 %shard_map.50 = (f32[1024,2048]{1,0:T(8,128)S(1)}, f32[16,8,128]{2,1,0:T(8,128)S(1)}) custom-call(bf16[1024,256]{1,0:T(8,128)(2,1)S(1)} %all_gather.6.raw_ref, bf16[2048,256]{1,0:T(8,128)(2,1)S(1)} %bitcast.6), custom_call_target="tpu_custom_call" | custom-call | tf_op jit(solution)/shard_map/pallas_call | solution.py:209
  45.1 20.1 %all_to_all.25.parts_ref = f32[16,8,128]{2,1,0:T(8,128)S(1)} all-to-all(f32[16,8,128]{2,1,0:T(8,128)S(1)} %get-tuple-element.16), channel_id=1, replica_groups=mesh['zh'=8,'zl'=2,'core'=2,'y'=4,'x'=4] {'zh','core'}, dimensions={0} | all-to-all | bytes 131072 | tf_op jit(solution)/shard_map/all_to_all | solution.py:243
  65.2 2.1 %shard_map.51 = (f32[8,128]{1,0:T(8,128)S(1)}, f32[1024,128]{1,0:T(8,128)S(1)}, f32[32,16,128]{2,1,0:T(8,128)S(1)}) custom-call(f32[16,8,128]{2,1,0:T(8,128)S(1)} %all_to_all.25.parts_ref, f32[1024,2048]{1,0:T(8,128)S(1)} %get-tuple-element.17.inner_ref), custom_call_target="tpu_custom_call" | custom-call | tf_op jit(solution)/shard_map/pallas_call | solution.py:209
  67.3 16.5 %all_to_all.26.parts_ref = f32[32,16,128]{2,1,0:T(8,128)S(1)} all-to-all(f32[32,16,128]{2,1,0:T(8,128)S(1)} %get-tuple-element.18), channel_id=1, replica_groups=mesh['zh'=8,'zl'=2,'core'=2,'y'=4,'x'=4] {'y','x','zl'}, dimensions={0} | all-to-all | bytes 524288 | tf_op jit(solution)/shard_map/all_to_all | solution.py:251
  83.8 1.3 %shard_map.52 = (f32[16,128]{1,0:T(8,128)S(1)}, f32[1024,2048]{1,0:T(8,128)S(1)}, bf16[128,128]{1,0:T(8,128)(2,1)S(1)}) custom-call(f32[32,16,128]{2,1,0:T(8,128)S(1)} %all_to_all.26.parts_ref, f32[1024,128]{1,0:T(8,128)S(1)} %get-tuple-element.19.column_ref, f32[1024,2048]{1,0:T(8,128)S(1)} %get-tuple-element.17.inner_ref), custom_call_target="tpu_custom_call" | custom-call | tf_op jit(solution)/shard_map/pallas_call | solution.py:209
  85.1 15.7 %all_to_all.27 = bf16[16,8,128]{2,1,0:T(8,128)(2,1)S(1)} all-to-all(bf16[16,8,128]{2,1,0:T(8,128)(2,1)S(1)} %bitcast.8), channel_id=1, replica_groups=mesh['zh'=8,'zl'=2,'core'=2,'y'=4,'x'=4] {'zh','core'}, dimensions={0} | all-to-all | bytes 65536 | tf_op jit(solution)/shard_map/all_to_all | solution.py:261
  100.8 1.7 %shard_map.53 = (f32[8,128]{1,0:T(8,128)S(1)}, f32[32,1,128]{2,1,0:T(1,128)S(1)}) custom-call(bf16[128,128]{1,0:T(8,128)(2,1)S(1)} %bitcast.7, f32[8,128]{1,0:T(8,128)S(1)} %get-tuple-element.21.phi_ref, f32[1024,2048]{1,0:T(8,128)S(1)} %get-tuple-element.22.plan_ref, f32[1024,2048]{1,0:T(8,128)S(1)} %get-tuple-element.17.inner_ref), custom_call_target="tpu_custom_call" | custom-call | tf_op jit(solution)/shard_map/pallas_call | solution.py:209
  102.6 10.3 %all_to_all.28.sums_ref = f32[32,1,128]{2,1,0:T(1,128)S(1)} all-to-all(f32[32,1,128]{2,1,0:T(1,128)S(1)} %get-tuple-element.23), channel_id=1, replica_groups=mesh['zh'=8,'zl'=2,'core'=2,'y'=4,'x'=4] {'y','x','zl'}, dimensions={0} | all-to-all | bytes 32768 | tf_op jit(solution)/shard_map/all_to_all | solution.py:272
  112.8 0.6 shard_map.54
Async XLA Ops:
  6.5 36.3 %all-to-all-start = ((bf16[16,128,256]{2,1,0:T(8,128)(2,1)}), bf16[16,128,256]{2,1,0:T(8,128)(2,1)S(1)}, u32[]{:S(2)}, u32[]{:S(2)}) async-start(bf16[16,128,256]{2,1,0:T(8,128)(2,1)} %shard_map.49), calls=%async_computation | async-start | bytes 2097152 | tf_op jit(solution)/shard_map/all_to_all | solution.py:233

commit v9 on v8

--- a/solution.py
+++ b/solution.py
@@ -49,18 +49,14 @@
         column_ref[block * LANES : (block + 1) * LANES] = wide.T
 
 
-def prepare_kernel(pair_ref, pair_out):
-    pair = normalize(pair_ref[...])
-    for peer in range(pair_out.shape[0]):
-        pair_out[peer] = pair
-
-
 def row_lse_kernel(
-    raw_ref, rollout_ref, inner_ref, out_ref, demo_ref, top_ref, total_ref
+    raw_ref, raw_rollout_ref, inner_ref, out_ref, demo_ref, rollout_ref, top_ref, total_ref
 ):
     rows, chunks = inner_ref.shape[0], inner_ref.shape[1] // LANES
     for row in range(0, rows, LANES):
         demo_ref[row : row + LANES] = normalize(raw_ref[row : row + LANES])
+    for row in range(0, raw_rollout_ref.shape[0], LANES):
+        rollout_ref[row : row + LANES] = normalize(raw_rollout_ref[row : row + LANES])
     for c in range(chunks // 2):
         inner = inner_of(demo_ref[...], rollout_ref[c * CHUNK : (c + 1) * CHUNK]) * SCALE
         inner_ref[:, c * CHUNK : (c + 1) * CHUNK] = inner
@@ -229,14 +225,19 @@
     column = pltpu.VMEM((rows, LANES), f32)
 
     pair = lax.all_gather(rollout, "zl", axis=0, tiled=True)
-    pairs = call(prepare_kernel, shape((n_plane, 2 * share, width), bf16), [], pair)
+    pairs = jnp.broadcast_to(pair[None], (n_plane, 2 * share, width))
     rollout_unit = lax.all_to_all(pairs, PLANE, 0, 0, tiled=True).reshape(cols, width)
     demo_unit = lax.all_gather(demo, LINE, axis=0, tiled=True)
 
     inner, row_parts = call(
         row_lse_kernel,
         (tile, shape((n_line,) + row_vec, f32)),
-        [pltpu.VMEM((rows, width), bf16), column, column],
+        [
+            pltpu.VMEM((rows, width), bf16),
+            pltpu.VMEM((cols, width), bf16),
+            column,
+            column,
+        ],
         demo_unit,
         rollout_unit,
     )
@@ -248,7 +249,7 @@
         row_parts,
         inner,
     )
-    col_parts = lax.all_to_all(col_parts, SHEET, 0, 0, tiled=True)
+    col_parts = lax.all_to_all(col_parts, SHEET[::-1], 0, 0, tiled=True)
     gamma, plan, row_parts = call(
         functools.partial(row_sum_kernel, log_cols),
         (shape(col_vec, f32), tile, shape((n_line * row_vec[0], LANES), bf16)),

time: 114 us -> 114 us (level)
    pallas_call x6 -> x5, Pallas kernels: 9.36 us -> 8.29 us  [call(): pl.pallas_call(kernel, out_shape=outs, in_specs=[VMEM] * len(args), out_s...]
where the time goes in v9:
time: 114 us; the launch traced here: 113 us
  blocking collectives  96.7 us (85%)
  Pallas kernels  8.29 us (7%)
  starting transfers between devices  6.75 us (6%)
    all_to_all x2, blocking collectives, body(): row_parts = lax.all_to_all(row_parts, LINE, 0, 0, tiled=True)  35.9 us
    all_gather x1, blocking collectives, body(): demo_unit = lax.all_gather(demo, LINE, axis=0, tiled=True)  29.5 us
    all_to_all x1, blocking collectives, body(): col_parts = lax.all_to_all(col_parts, SHEET[::-1], 0, 0, tiled=True)  16 us
    all_to_all x1, blocking collectives, body(): sums = lax.all_to_all(sums, SHEET, 0, 0, tiled=True)  10.5 us
    pallas_call x5, Pallas kernels, call(): pl.pallas_call(kernel, out_shape=outs, in_specs=[VMEM] * len(args), out_s...  8.29 us
    all_to_all x1, starting transfers between devices, body(): lax.all_to_all(pairs, PLANE, 0, 0, tiled=True).reshape(cols, width)  6.75 us
    all_gather x1, blocking collectives, body(): pair = lax.all_gather(rollout, 'zl', axis=0, tiled=True)  4.7 us
  transfers between devices with their start and end apart: 1, of which 0 were waited for; matrix products, arithmetic and copies ran while one was open for 0% of the time, Pallas kernels for 0%

profile of v9, /device:TPU:1, one launch (start us, length us, event | category | flops | bytes accessed | tf_op | source)
XLA Modules:
  0.0 113.4 jit_solution(13787391758101231235)
XLA Ops:
  0.6 4.7 %all_gather.7 = bf16[128,256]{1,0:T(8,128)(2,1)S(1)} all-gather(bf16[64,256]{1,0:T(8,128)(2,1)} %param.3), channel_id=1, replica_groups=mesh['zh'=8,'zl'=2,'core'=2,'y'=4,'x'=4] {'zl'}, dimensions={0}, use_global_device_ids=true | all-gather | bytes 98304 | tf_op jit(solution)/shard_map/all_gather | solution.py:227
  5.3 1.1 broadcast_in_dim.2
  6.4 6.8 %all-to-all-start = ((bf16[16,128,256]{2,1,0:T(8,128)(2,1)}), bf16[16,128,256]{2,1,0:T(8,128)(2,1)S(1)}, u32[]{:S(2)}, u32[]{:S(2)}) async-start(bf16[16,128,256]{2,1,0:T(8,128)(2,1)} %broadcast_in_dim.2), calls=%async_computation | async-start | bytes 2097152 | tf_op jit(solution)/shard_map/all_to_all | solution.py:229
  13.2 29.5 %all_gather.6.raw_ref = bf16[1024,256]{1,0:T(8,128)(2,1)S(1)} all-gather(bf16[64,256]{1,0:T(8,128)(2,1)} %param.2), channel_id=1, replica_groups=mesh['zh'=8,'zl'=2,'core'=2,'y'=4,'x'=4] {'zh','core'}, dimensions={0}, use_global_device_ids=true | all-gather | bytes 557056 | tf_op jit(solution)/shard_map/all_gather | solution.py:230
  42.7 0.0 all-to-all-done
  42.7 2.5 %shard_map.49 = (f32[1024,2048]{1,0:T(8,128)S(1)}, f32[16,8,128]{2,1,0:T(8,128)S(1)}) custom-call(bf16[1024,256]{1,0:T(8,128)(2,1)S(1)} %all_gather.6.raw_ref, bf16[2048,256]{1,0:T(8,128)(2,1)S(1)} %bitcast.6), custom_call_target="tpu_custom_call" | custom-call | tf_op jit(solution)/shard_map/pallas_call | solution.py:205
  45.1 20.1 %all_to_all.25.parts_ref = f32[16,8,128]{2,1,0:T(8,128)S(1)} all-to-all(f32[16,8,128]{2,1,0:T(8,128)S(1)} %get-tuple-element.16), channel_id=1, replica_groups=mesh['zh'=8,'zl'=2,'core'=2,'y'=4,'x'=4] {'zh','core'}, dimensions={0} | all-to-all | bytes 131072 | tf_op jit(solution)/shard_map/all_to_all | solution.py:244
  65.2 2.1 %shard_map.50 = (f32[8,128]{1,0:T(8,128)S(1)}, f32[1024,128]{1,0:T(8,128)S(1)}, f32[32,16,128]{2,1,0:T(8,128)S(1)}) custom-call(f32[16,8,128]{2,1,0:T(8,128)S(1)} %all_to_all.25.parts_ref, f32[1024,2048]{1,0:T(8,128)S(1)} %get-tuple-element.17.inner_ref), custom_call_target="tpu_custom_call" | custom-call | tf_op jit(solution)/shard_map/pallas_call | solution.py:205
  67.3 16.0 %all_to_all.26.parts_ref = f32[32,16,128]{2,1,0:T(8,128)S(1)} all-to-all(f32[32,16,128]{2,1,0:T(8,128)S(1)} %get-tuple-element.18), channel_id=1, replica_groups=mesh['zh'=8,'zl'=2,'core'=2,'y'=4,'x'=4] {'zl','x','y'}, dimensions={0} | all-to-all | bytes 524288 | tf_op jit(solution)/shard_map/all_to_all | solution.py:252
  83.4 1.3 %shard_map.51 = (f32[16,128]{1,0:T(8,128)S(1)}, f32[1024,2048]{1,0:T(8,128)S(1)}, bf16[128,128]{1,0:T(8,128)(2,1)S(1)}) custom-call(f32[32,16,128]{2,1,0:T(8,128)S(1)} %all_to_all.26.parts_ref, f32[1024,128]{1,0:T(8,128)S(1)} %get-tuple-element.19.column_ref, f32[1024,2048]{1,0:T(8,128)S(1)} %get-tuple-element.17.inner_ref), custom_call_target="tpu_custom_call" | custom-call | tf_op jit(solution)/shard_map/pallas_call | solution.py:205
  84.7 15.8 %all_to_all.27 = bf16[16,8,128]{2,1,0:T(8,128)(2,1)S(1)} all-to-all(bf16[16,8,128]{2,1,0:T(8,128)(2,1)S(1)} %bitcast.8), channel_id=1, replica_groups=mesh['zh'=8,'zl'=2,'core'=2,'y'=4,'x'=4] {'zh','core'}, dimensions={0} | all-to-all | bytes 65536 | tf_op jit(solution)/shard_map/all_to_all | solution.py:262
  100.5 1.7 %shard_map.52 = (f32[8,128]{1,0:T(8,128)S(1)}, f32[32,1,128]{2,1,0:T(1,128)S(1)}) custom-call(bf16[128,128]{1,0:T(8,128)(2,1)S(1)} %bitcast.7, f32[8,128]{1,0:T(8,128)S(1)} %get-tuple-element.21.phi_ref, f32[1024,2048]{1,0:T(8,128)S(1)} %get-tuple-element.22.plan_ref, f32[1024,2048]{1,0:T(8,128)S(1)} %get-tuple-element.17.inner_ref), custom_call_target="tpu_custom_call" | custom-call | tf_op jit(solution)/shard_map/pallas_call | solution.py:205
  102.3 10.5 %all_to_all.28.sums_ref = f32[32,1,128]{2,1,0:T(1,128)S(1)} all-to-all(f32[32,1,128]{2,1,0:T(1,128)S(1)} %get-tuple-element.23), channel_id=1, replica_groups=mesh['zh'=8,'zl'=2,'core'=2,'y'=4,'x'=4] {'y','x','zl'}, dimensions={0} | all-to-all | bytes 32768 | tf_op jit(solution)/shard_map/all_to_all | solution.py:273
  112.8 0.6 shard_map.53
Async XLA Ops:
  6.4 36.3 %all-to-all-start = ((bf16[16,128,256]{2,1,0:T(8,128)(2,1)}), bf16[16,128,256]{2,1,0:T(8,128)(2,1)S(1)}, u32[]{:S(2)}, u32[]{:S(2)}) async-start(bf16[16,128,256]{2,1,0:T(8,128)(2,1)} %broadcast_in_dim.2), calls=%async_computation | async-start | bytes 2097152 | tf_op jit(solution)/shard_map/all_to_all | solution.py:229

commit v10 on v9

--- a/solution.py
+++ b/solution.py
@@ -13,7 +13,7 @@
 SCALE = 1.0 / (EPS * math.log(2.0))
 LN2 = math.log(2.0)
 LANES = 128
-CHUNK = 256
+CHUNK = 512
 PLANE = ("y", "x")
 SHEET = ("y", "x", "zl")
 LINE = ("zh", "core")
@@ -57,10 +57,10 @@
         demo_ref[row : row + LANES] = normalize(raw_ref[row : row + LANES])
     for row in range(0, raw_rollout_ref.shape[0], LANES):
         rollout_ref[row : row + LANES] = normalize(raw_rollout_ref[row : row + LANES])
-    for c in range(chunks // 2):
+    for c in range(chunks * LANES // CHUNK):
         inner = inner_of(demo_ref[...], rollout_ref[c * CHUNK : (c + 1) * CHUNK]) * SCALE
         inner_ref[:, c * CHUNK : (c + 1) * CHUNK] = inner
-        peak = jnp.maximum(inner[:, :LANES], inner[:, LANES:])
+        peak = fold(jnp.maximum, [inner[:, lanes(k)] for k in range(CHUNK // LANES)])
         top_ref[...] = peak if c == 0 else jnp.maximum(top_ref[...], peak)
 
     for row in range(0, rows, 64):

time: 114 us -> 114 us (level)
  no operation moved by 1% of the time
where the time goes in v10:
time: 114 us; the launch traced here: 113 us
  blocking collectives  96.7 us (85%)
  Pallas kernels  8.29 us (7%)
  starting transfers between devices  6.75 us (6%)
    all_to_all x2, blocking collectives, body(): row_parts = lax.all_to_all(row_parts, LINE, 0, 0, tiled=True)  35.9 us
    all_gather x1, blocking collectives, body(): demo_unit = lax.all_gather(demo, LINE, axis=0, tiled=True)  29.5 us
    all_to_all x1, blocking collectives, body(): col_parts = lax.all_to_all(col_parts, SHEET[::-1], 0, 0, tiled=True)  16 us
    all_to_all x1, blocking collectives, body(): sums = lax.all_to_all(sums, SHEET, 0, 0, tiled=True)  10.5 us
    pallas_call x5, Pallas kernels, call(): pl.pallas_call(kernel, out_shape=outs, in_specs=[VMEM] * len(args), out_s...  8.29 us
    all_to_all x1, starting transfers between devices, body(): lax.all_to_all(pairs, PLANE, 0, 0, tiled=True).reshape(cols, width)  6.75 us
    all_gather x1, blocking collectives, body(): pair = lax.all_gather(rollout, 'zl', axis=0, tiled=True)  4.7 us
  transfers between devices with their start and end apart: 1, of which 0 were waited for; matrix products, arithmetic and copies ran while one was open for 0% of the time, Pallas kernels for 0%

profile of v10, /device:TPU:1, one launch (start us, length us, event | category | flops | bytes accessed | tf_op | source)
XLA Modules:
  0.0 113.4 jit_solution(18016649624239496940)
XLA Ops:
  0.6 4.7 %all_gather.7 = bf16[128,256]{1,0:T(8,128)(2,1)S(1)} all-gather(bf16[64,256]{1,0:T(8,128)(2,1)} %param.3), channel_id=1, replica_groups=mesh['zh'=8,'zl'=2,'core'=2,'y'=4,'x'=4] {'zl'}, dimensions={0}, use_global_device_ids=true | all-gather | bytes 98304 | tf_op jit(solution)/shard_map/all_gather | solution.py:227
  5.3 1.1 broadcast_in_dim.2
  6.4 6.8 %all-to-all-start = ((bf16[16,128,256]{2,1,0:T(8,128)(2,1)}), bf16[16,128,256]{2,1,0:T(8,128)(2,1)S(1)}, u32[]{:S(2)}, u32[]{:S(2)}) async-start(bf16[16,128,256]{2,1,0:T(8,128)(2,1)} %broadcast_in_dim.2), calls=%async_computation | async-start | bytes 2097152 | tf_op jit(solution)/shard_map/all_to_all | solution.py:229
  13.2 29.5 %all_gather.6.raw_ref = bf16[1024,256]{1,0:T(8,128)(2,1)S(1)} all-gather(bf16[64,256]{1,0:T(8,128)(2,1)} %param.2), channel_id=1, replica_groups=mesh['zh'=8,'zl'=2,'core'=2,'y'=4,'x'=4] {'zh','core'}, dimensions={0}, use_global_device_ids=true | all-gather | bytes 557056 | tf_op jit(solution)/shard_map/all_gather | solution.py:230
  42.7 0.0 all-to-all-done
  42.7 2.5 %shard_map.49 = (f32[1024,2048]{1,0:T(8,128)S(1)}, f32[16,8,128]{2,1,0:T(8,128)S(1)}) custom-call(bf16[1024,256]{1,0:T(8,128)(2,1)S(1)} %all_gather.6.raw_ref, bf16[2048,256]{1,0:T(8,128)(2,1)S(1)} %bitcast.6), custom_call_target="tpu_custom_call" | custom-call | tf_op jit(solution)/shard_map/pallas_call | solution.py:205
  45.1 20.1 %all_to_all.25.parts_ref = f32[16,8,128]{2,1,0:T(8,128)S(1)} all-to-all(f32[16,8,128]{2,1,0:T(8,128)S(1)} %get-tuple-element.16), channel_id=1, replica_groups=mesh['zh'=8,'zl'=2,'core'=2,'y'=4,'x'=4] {'zh','core'}, dimensions={0} | all-to-all | bytes 131072 | tf_op jit(solution)/shard_map/all_to_all | solution.py:244
  65.2 2.1 %shard_map.50 = (f32[8,128]{1,0:T(8,128)S(1)}, f32[1024,128]{1,0:T(8,128)S(1)}, f32[32,16,128]{2,1,0:T(8,128)S(1)}) custom-call(f32[16,8,128]{2,1,0:T(8,128)S(1)} %all_to_all.25.parts_ref, f32[1024,2048]{1,0:T(8,128)S(1)} %get-tuple-element.17.inner_ref), custom_call_target="tpu_custom_call" | custom-call | tf_op jit(solution)/shard_map/pallas_call | solution.py:205
  67.4 16.0 %all_to_all.26.parts_ref = f32[32,16,128]{2,1,0:T(8,128)S(1)} all-to-all(f32[32,16,128]{2,1,0:T(8,128)S(1)} %get-tuple-element.18), channel_id=1, replica_groups=mesh['zh'=8,'zl'=2,'core'=2,'y'=4,'x'=4] {'zl','x','y'}, dimensions={0} | all-to-all | bytes 524288 | tf_op jit(solution)/shard_map/all_to_all | solution.py:252
  83.4 1.3 %shard_map.51 = (f32[16,128]{1,0:T(8,128)S(1)}, f32[1024,2048]{1,0:T(8,128)S(1)}, bf16[128,128]{1,0:T(8,128)(2,1)S(1)}) custom-call(f32[32,16,128]{2,1,0:T(8,128)S(1)} %all_to_all.26.parts_ref, f32[1024,128]{1,0:T(8,128)S(1)} %get-tuple-element.19.column_ref, f32[1024,2048]{1,0:T(8,128)S(1)} %get-tuple-element.17.inner_ref), custom_call_target="tpu_custom_call" | custom-call | tf_op jit(solution)/shard_map/pallas_call | solution.py:205
  84.7 15.8 %all_to_all.27 = bf16[16,8,128]{2,1,0:T(8,128)(2,1)S(1)} all-to-all(bf16[16,8,128]{2,1,0:T(8,128)(2,1)S(1)} %bitcast.8), channel_id=1, replica_groups=mesh['zh'=8,'zl'=2,'core'=2,'y'=4,'x'=4] {'zh','core'}, dimensions={0} | all-to-all | bytes 65536 | tf_op jit(solution)/shard_map/all_to_all | solution.py:262
  100.6 1.7 %shard_map.52 = (f32[8,128]{1,0:T(8,128)S(1)}, f32[32,1,128]{2,1,0:T(1,128)S(1)}) custom-call(bf16[128,128]{1,0:T(8,128)(2,1)S(1)} %bitcast.7, f32[8,128]{1,0:T(8,128)S(1)} %get-tuple-element.21.phi_ref, f32[1024,2048]{1,0:T(8,128)S(1)} %get-tuple-element.22.plan_ref, f32[1024,2048]{1,0:T(8,128)S(1)} %get-tuple-element.17.inner_ref), custom_call_target="tpu_custom_call" | custom-call | tf_op jit(solution)/shard_map/pallas_call | solution.py:205
  102.3 10.5 %all_to_all.28.sums_ref = f32[32,1,128]{2,1,0:T(1,128)S(1)} all-to-all(f32[32,1,128]{2,1,0:T(1,128)S(1)} %get-tuple-element.23), channel_id=1, replica_groups=mesh['zh'=8,'zl'=2,'core'=2,'y'=4,'x'=4] {'y','x','zl'}, dimensions={0} | all-to-all | bytes 32768 | tf_op jit(solution)/shard_map/all_to_all | solution.py:273
  112.8 0.6 shard_map.53
Async XLA Ops:
  6.4 36.3 %all-to-all-start = ((bf16[16,128,256]{2,1,0:T(8,128)(2,1)}), bf16[16,128,256]{2,1,0:T(8,128)(2,1)S(1)}, u32[]{:S(2)}, u32[]{:S(2)}) async-start(bf16[16,128,256]{2,1,0:T(8,128)(2,1)} %broadcast_in_dim.2), calls=%async_computation | async-start | bytes 2097152 | tf_op jit(solution)/shard_map/all_to_all | solution.py:229

commit v11 on v9

--- a/solution.py
+++ b/solution.py
@@ -156,7 +156,7 @@
     phi_out[...] = phi_ref[...] + change
     spread_rows(jnp.exp2(change), column_ref)
     rows, chunks = plan_ref.shape[0], plan_ref.shape[1] // LANES
-    step = 128
+    step = 256
 
     def add_up(b, totals):
         totals = list(totals)

time: 114 us -> 114 us (level)
  no operation moved by 1% of the time
where the time goes in v11:
time: 114 us; the launch traced here: 113 us
  blocking collectives  96.7 us (85%)
  Pallas kernels  8.26 us (7%)
  starting transfers between devices  6.75 us (6%)
    all_to_all x2, blocking collectives, body(): row_parts = lax.all_to_all(row_parts, LINE, 0, 0, tiled=True)  35.9 us
    all_gather x1, blocking collectives, body(): demo_unit = lax.all_gather(demo, LINE, axis=0, tiled=True)  29.5 us
    all_to_all x1, blocking collectives, body(): col_parts = lax.all_to_all(col_parts, SHEET[::-1], 0, 0, tiled=True)  16 us
    all_to_all x1, blocking collectives, body(): sums = lax.all_to_all(sums, SHEET, 0, 0, tiled=True)  10.5 us
    pallas_call x5, Pallas kernels, call(): pl.pallas_call(kernel, out_shape=outs, in_specs=[VMEM] * len(args), out_s...  8.26 us
    all_to_all x1, starting transfers between devices, body(): lax.all_to_all(pairs, PLANE, 0, 0, tiled=True).reshape(cols, width)  6.75 us
    all_gather x1, blocking collectives, body(): pair = lax.all_gather(rollout, 'zl', axis=0, tiled=True)  4.7 us
  transfers between devices with their start and end apart: 1, of which 0 were waited for; matrix products, arithmetic and copies ran while one was open for 0% of the time, Pallas kernels for 0%

profile of v11, /device:TPU:1, one launch (start us, length us, event | category | flops | bytes accessed | tf_op | source)
XLA Modules:
  0.0 113.4 jit_solution(14953011421079705111)
XLA Ops:
  0.6 4.7 %all_gather.7 = bf16[128,256]{1,0:T(8,128)(2,1)S(1)} all-gather(bf16[64,256]{1,0:T(8,128)(2,1)} %param.3), channel_id=1, replica_groups=mesh['zh'=8,'zl'=2,'core'=2,'y'=4,'x'=4] {'zl'}, dimensions={0}, use_global_device_ids=true | all-gather | bytes 98304 | tf_op jit(solution)/shard_map/all_gather | solution.py:227
  5.3 1.1 broadcast_in_dim.2
  6.4 6.8 %all-to-all-start = ((bf16[16,128,256]{2,1,0:T(8,128)(2,1)}), bf16[16,128,256]{2,1,0:T(8,128)(2,1)S(1)}, u32[]{:S(2)}, u32[]{:S(2)}) async-start(bf16[16,128,256]{2,1,0:T(8,128)(2,1)} %broadcast_in_dim.2), calls=%async_computation | async-start | bytes 2097152 | tf_op jit(solution)/shard_map/all_to_all | solution.py:229
  13.2 29.5 %all_gather.6.raw_ref = bf16[1024,256]{1,0:T(8,128)(2,1)S(1)} all-gather(bf16[64,256]{1,0:T(8,128)(2,1)} %param.2), channel_id=1, replica_groups=mesh['zh'=8,'zl'=2,'core'=2,'y'=4,'x'=4] {'zh','core'}, dimensions={0}, use_global_device_ids=true | all-gather | bytes 557056 | tf_op jit(solution)/shard_map/all_gather | solution.py:230
  42.7 0.0 all-to-all-done
  42.7 2.5 %shard_map.49 = (f32[1024,2048]{1,0:T(8,128)S(1)}, f32[16,8,128]{2,1,0:T(8,128)S(1)}) custom-call(bf16[1024,256]{1,0:T(8,128)(2,1)S(1)} %all_gather.6.raw_ref, bf16[2048,256]{1,0:T(8,128)(2,1)S(1)} %bitcast.6), custom_call_target="tpu_custom_call" | custom-call | tf_op jit(solution)/shard_map/pallas_call | solution.py:205
  45.1 20.1 %all_to_all.25.parts_ref = f32[16,8,128]{2,1,0:T(8,128)S(1)} all-to-all(f32[16,8,128]{2,1,0:T(8,128)S(1)} %get-tuple-element.16), channel_id=1, replica_groups=mesh['zh'=8,'zl'=2,'core'=2,'y'=4,'x'=4] {'zh','core'}, dimensions={0} | all-to-all | bytes 131072 | tf_op jit(solution)/shard_map/all_to_all | solution.py:244
  65.2 2.1 %shard_map.50 = (f32[8,128]{1,0:T(8,128)S(1)}, f32[1024,128]{1,0:T(8,128)S(1)}, f32[32,16,128]{2,1,0:T(8,128)S(1)}) custom-call(f32[16,8,128]{2,1,0:T(8,128)S(1)} %all_to_all.25.parts_ref, f32[1024,2048]{1,0:T(8,128)S(1)} %get-tuple-element.17.inner_ref), custom_call_target="tpu_custom_call" | custom-call | tf_op jit(solution)/shard_map/pallas_call | solution.py:205
  67.3 16.0 %all_to_all.26.parts_ref = f32[32,16,128]{2,1,0:T(8,128)S(1)} all-to-all(f32[32,16,128]{2,1,0:T(8,128)S(1)} %get-tuple-element.18), channel_id=1, replica_groups=mesh['zh'=8,'zl'=2,'core'=2,'y'=4,'x'=4] {'zl','x','y'}, dimensions={0} | all-to-all | bytes 524288 | tf_op jit(solution)/shard_map/all_to_all | solution.py:252
  83.4 1.3 %shard_map.51 = (f32[16,128]{1,0:T(8,128)S(1)}, f32[1024,2048]{1,0:T(8,128)S(1)}, bf16[128,128]{1,0:T(8,128)(2,1)S(1)}) custom-call(f32[32,16,128]{2,1,0:T(8,128)S(1)} %all_to_all.26.parts_ref, f32[1024,128]{1,0:T(8,128)S(1)} %get-tuple-element.19.column_ref, f32[1024,2048]{1,0:T(8,128)S(1)} %get-tuple-element.17.inner_ref), custom_call_target="tpu_custom_call" | custom-call | tf_op jit(solution)/shard_map/pallas_call | solution.py:205
  84.7 15.8 %all_to_all.27 = bf16[16,8,128]{2,1,0:T(8,128)(2,1)S(1)} all-to-all(bf16[16,8,128]{2,1,0:T(8,128)(2,1)S(1)} %bitcast.8), channel_id=1, replica_groups=mesh['zh'=8,'zl'=2,'core'=2,'y'=4,'x'=4] {'zh','core'}, dimensions={0} | all-to-all | bytes 65536 | tf_op jit(solution)/shard_map/all_to_all | solution.py:262
  100.5 1.7 %shard_map.52 = (f32[8,128]{1,0:T(8,128)S(1)}, f32[32,1,128]{2,1,0:T(1,128)S(1)}) custom-call(bf16[128,128]{1,0:T(8,128)(2,1)S(1)} %bitcast.7, f32[8,128]{1,0:T(8,128)S(1)} %get-tuple-element.21.phi_ref, f32[1024,2048]{1,0:T(8,128)S(1)} %get-tuple-element.22.plan_ref, f32[1024,2048]{1,0:T(8,128)S(1)} %get-tuple-element.17.inner_ref), custom_call_target="tpu_custom_call" | custom-call | tf_op jit(solution)/shard_map/pallas_call | solution.py:205
  102.3 10.5 %all_to_all.28.sums_ref = f32[32,1,128]{2,1,0:T(1,128)S(1)} all-to-all(f32[32,1,128]{2,1,0:T(1,128)S(1)} %get-tuple-element.23), channel_id=1, replica_groups=mesh['zh'=8,'zl'=2,'core'=2,'y'=4,'x'=4] {'y','x','zl'}, dimensions={0} | all-to-all | bytes 32768 | tf_op jit(solution)/shard_map/all_to_all | solution.py:273
  112.8 0.6 shard_map.53
Async XLA Ops:
  6.4 36.3 %all-to-all-start = ((bf16[16,128,256]{2,1,0:T(8,128)(2,1)}), bf16[16,128,256]{2,1,0:T(8,128)(2,1)S(1)}, u32[]{:S(2)}, u32[]{:S(2)}) async-start(bf16[16,128,256]{2,1,0:T(8,128)(2,1)} %broadcast_in_dim.2), calls=%async_computation | async-start | bytes 2097152 | tf_op jit(solution)/shard_map/all_to_all | solution.py:229
